TPU v7x, 32 devices: a whole 2x2x4 slice. The times are simulated.
32 devices in a mesh: dp: 4 (over z), mp: 8 (over y, x, core).
Axes of the slice: x: 2, y: 2, z: 4, core: 2. Of those that a mesh axis runs over, the one named last changes fastest.
Arguments:
- tokens: bfloat16 [12288, 1024], P(('dp', 'mp')), may hold values from -6 to 6
- lengths: int32 [96], P('dp'), may hold values from 16 to 128, as said below
- student_qkv: float32 [1024, 3, 1024], P(None, None, 'mp'), may hold values from -0.1875 to 0.1875
- student_qv_bias: bfloat16 [2, 1024], P(None, 'mp'), may hold values from -3 to 3
- student_out: float32 [1024, 1024], P('mp'), may hold values from -0.5 to 0.5
- student_up: float32 [1024, 4096], P(None, 'mp'), may hold values from -0.1875 to 0.1875
- student_up_bias: bfloat16 [4096], P('mp'), may hold values from -3 to 3
- student_down: float32 [4096, 1024], P('mp'), may hold values from -0.09375 to 0.09375
- student_out_bias: bfloat16 [2, 1024], replicated, may hold values from -3 to 3
- student_gain: bfloat16 [2, 1024], replicated, may hold values from 0.25 to 1.75
- student_shift: bfloat16 [2, 1024], replicated, may hold values from -3 to 3
- teacher_qkv: bfloat16 [1024, 3, 1024], P(None, None, 'mp'), may hold values from -0.1875 to 0.1875
- teacher_qv_bias: bfloat16 [2, 1024], P(None, 'mp'), may hold values from -3 to 3
- teacher_out: bfloat16 [1024, 1024], P('mp'), may hold values from -0.5 to 0.5
- teacher_up: bfloat16 [1024, 4096], P(None, 'mp'), may hold values from -0.1875 to 0.1875
- teacher_up_bias: bfloat16 [4096], P('mp'), may hold values from -3 to 3
- teacher_down: bfloat16 [4096, 1024], P('mp'), may hold values from -0.09375 to 0.09375
- teacher_out_bias: bfloat16 [2, 1024], replicated, may hold values from -3 to 3
- teacher_gain: bfloat16 [2, 1024], replicated, may hold values from 0.25 to 1.75
- teacher_shift: bfloat16 [2, 1024], replicated, may hold values from -3 to 3
Outputs:
- student_output: bfloat16 [12288, 1024], P(('dp', 'mp'))
- input_grad: float32 [12288, 1024], P(('dp', 'mp'))
- grad_qkv: float32 [1024, 3, 1024], P(None, None, 'mp')
- grad_qv_bias: float32 [2, 1024], P(None, 'mp')
- grad_out: float32 [1024, 1024], P('mp')
- grad_up: float32 [1024, 4096], P(None, 'mp')
- grad_up_bias: float32 [4096], P('mp')
- grad_down: float32 [4096, 1024], P('mp')
- grad_out_bias: float32 [2, 1024], replicated
- grad_gain: float32 [2, 1024], replicated
- grad_shift: float32 [2, 1024], replicated
Inputs may be any that keep to these rules, and one draw needn't show every extreme that they name: `lengths`: the true length of each sentence pair; pairs are in groups of five starting at indices that are multiples of five; in each group the first pair has length 128 and the third 128 // 8.
All inputs are finite; a program needn't handle non-finite values.
Results may differ from a plain program's by a relative error of at most 0.015.
Values may be sent and summed in bfloat16 or wider, within the bound.
A program may use at most 256 MiB of HBM per device.

v0:
```python
import math

import jax
import jax.numpy as jnp
from jax import lax
from jax.sharding import PartitionSpec as P

DH = 64
LEN = 128


norm_epsilon = 1e-06
clip_level = 2.5
score_weight = 0.05
masked_fill = -1000000000.0


def to_float(values):
    return values.astype(jnp.float32)


def binarize(matrix, axis_index):
    scaling = jnp.mean(jnp.abs(matrix), axis=axis_index, keepdims=True)
    return (scaling * jnp.sign(matrix)).astype(jnp.bfloat16)


def norm_affine(values, gain_row, shift_row):
    centred = values - jnp.mean(values, axis=-1, keepdims=True)
    variance = jnp.mean(centred * centred, axis=-1, keepdims=True)
    return centred * lax.rsqrt(variance + norm_epsilon) * gain_row + shift_row


def clipped_gelu(hidden):
    return clip_level * jnp.tanh(jax.nn.gelu(hidden, approximate=False) / clip_level)


def plain_gelu(hidden):
    return jax.nn.gelu(hidden, approximate=False)


def raw_scores(queries, key_rows, head_size):
    factor = 1.0 / math.sqrt(head_size)
    return (
        jnp.einsum("bqhe,bkhe->bhqk", queries, key_rows, preferred_element_type=jnp.float32)
        * factor
    )


def attend(gathered, qkv_weight, qv_bias, key_valid, head_size):
    total_rows = gathered.shape[0]
    features = qkv_weight.shape[0]
    head_cols = qkv_weight.shape[2]
    projected = jnp.dot(
        gathered, qkv_weight.reshape(features, 3 * head_cols), preferred_element_type=jnp.float32
    )
    projected = projected.reshape(total_rows, 3, head_cols)
    head_shape = (key_valid.shape[0], key_valid.shape[1], head_cols // head_size, head_size)
    queries = (projected[:, 0] + qv_bias[0]).astype(jnp.bfloat16).reshape(head_shape)
    key_rows = projected[:, 1].astype(jnp.bfloat16).reshape(head_shape)
    value_rows = (projected[:, 2] + qv_bias[1]).astype(jnp.bfloat16).reshape(head_shape)
    scores = raw_scores(queries, key_rows, head_size)
    masked = jnp.where(key_valid[:, None, None, :], scores, masked_fill)
    log_norm = jax.nn.logsumexp(masked, axis=-1, keepdims=True)
    attention = jnp.exp(masked - log_norm).astype(jnp.bfloat16)
    context = jnp.einsum(
        "bhqk,bkhe->bqhe", attention, value_rows, preferred_element_type=jnp.float32
    )
    context = context.astype(jnp.bfloat16).reshape(total_rows, head_cols)
    return (queries, key_rows, value_rows, log_norm, context)


def attend_back(
    queries, key_rows, value_rows, log_norm, context_grad, scores, score_extra, key_valid, head_size
):
    total_rows = context_grad.shape[0]
    head_cols = context_grad.shape[1]
    factor = 1.0 / math.sqrt(head_size)
    masked = jnp.where(key_valid[:, None, None, :], scores, masked_fill)
    attention = jnp.exp(masked - log_norm)
    grad_four = context_grad.reshape(queries.shape)
    attention_grad = jnp.einsum(
        "bqhe,bkhe->bhqk", grad_four, value_rows, preferred_element_type=jnp.float32
    )
    value_grad = jnp.einsum(
        "bhqk,bqhe->bkhe",
        attention.astype(jnp.bfloat16),
        grad_four,
        preferred_element_type=jnp.float32,
    )
    inner_sum = jnp.sum(attention * attention_grad, axis=-1, keepdims=True)
    score_grad = attention * (attention_grad - inner_sum) + score_extra
    score_low = score_grad.astype(jnp.bfloat16)
    query_grad = (
        jnp.einsum("bhqk,bkhe->bqhe", score_low, key_rows, preferred_element_type=jnp.float32)
        * factor
    )
    key_grad = (
        jnp.einsum("bhqk,bqhe->bkhe", score_low, queries, preferred_element_type=jnp.float32)
        * factor
    )
    return (
        query_grad.reshape(total_rows, head_cols),
        key_grad.reshape(total_rows, head_cols),
        value_grad.reshape(total_rows, head_cols),
    )


def feed_forward(ffn_input, up_weight, up_bias, down_weight, activation):
    pre_act = jnp.dot(ffn_input, up_weight, preferred_element_type=jnp.float32) + to_float(up_bias)
    hidden = activation(pre_act).astype(jnp.bfloat16)
    branch_part = jnp.dot(hidden, down_weight, preferred_element_type=jnp.float32)
    return (pre_act, hidden, branch_part)


def feed_back(branch_grad, pre_act, up_weight, down_weight, activation):
    hidden_grad = jnp.dot(branch_grad, down_weight.T, preferred_element_type=jnp.float32)
    unused, act_back = jax.vjp(activation, pre_act)
    pre_grad = act_back(hidden_grad)[0]
    pre_low = pre_grad.astype(jnp.bfloat16)
    input_part = jnp.dot(pre_low, up_weight.T, preferred_element_type=jnp.float32)
    return (pre_grad, pre_low, input_part)


def per_device(
    tokens,
    lengths,
    student_qkv,
    student_qv_bias,
    student_out,
    student_up,
    student_up_bias,
    student_down,
    student_out_bias,
    student_gain,
    student_shift,
    teacher_qkv,
    teacher_qv_bias,
    teacher_out,
    teacher_up,
    teacher_up_bias,
    teacher_down,
    teacher_out_bias,
    teacher_gain,
    teacher_shift,
):
    local_rows = tokens.shape[0]
    local_seqs = local_rows // LEN
    places = jnp.arange(LEN, dtype=jnp.int32)
    own_lengths = lax.dynamic_slice_in_dim(lengths, lax.axis_index("mp") * local_seqs, local_seqs)
    own_valid = places[None, :] < own_lengths[:, None]
    token_valid = own_valid.reshape(local_rows, 1).astype(jnp.float32)
    binary_qkv = binarize(student_qkv, 0)
    binary_out = binarize(student_out, 1)
    binary_up = binarize(student_up, 0)
    binary_down = binarize(student_down, 1)
    stud_out_bias = to_float(student_out_bias)
    stud_gain = to_float(student_gain)
    stud_shift = to_float(student_shift)
    teach_out_bias = to_float(teacher_out_bias)
    teach_gain = to_float(teacher_gain)
    teach_shift = to_float(teacher_shift)
    input_local = to_float(tokens)
    qkv_all, out_all, teach_qkv_all, teach_out_all, stud_qv_all, teach_qv_all = (
        binary_qkv,
        binary_out,
        teacher_qkv,
        teacher_out,
        student_qv_bias,
        teacher_qv_bias,
    )
    attn_rows = lax.all_gather(tokens, "mp", axis=0, tiled=True)
    key_valid = places[None, :] < lengths[:, None]
    pair_valid = key_valid[:, None, :, None] & key_valid[:, None, None, :]
    features = qkv_all.shape[0]
    head_cols = qkv_all.shape[2]
    stud_query, stud_key, stud_value, stud_lse, stud_context = attend(
        attn_rows, qkv_all, to_float(stud_qv_all), key_valid, DH
    )
    teach_query, teach_key, teach_value, teach_lse, teach_context = attend(
        attn_rows, teach_qkv_all, to_float(teach_qv_all), key_valid, DH
    )
    stud_attn_part = jnp.dot(stud_context, out_all, preferred_element_type=jnp.float32)
    teach_attn_part = jnp.dot(teach_context, teach_out_all, preferred_element_type=jnp.float32)
    stud_attended, teach_attended = (
        lax.psum_scatter(
            stud_attn_part.astype(jnp.bfloat16), "mp", scatter_dimension=0, tiled=True
        ).astype(jnp.float32),
        lax.psum_scatter(
            teach_attn_part.astype(jnp.bfloat16), "mp", scatter_dimension=0, tiled=True
        ).astype(jnp.float32),
    )
    stud_first = input_local + stud_attended + stud_out_bias[0]
    teach_first = input_local + teach_attended + teach_out_bias[0]
    stud_normed = norm_affine(stud_first, stud_gain[0], stud_shift[0])
    teach_normed = norm_affine(teach_first, teach_gain[0], teach_shift[0])
    stud_normed_low = stud_normed.astype(jnp.bfloat16)
    teach_normed_low = teach_normed.astype(jnp.bfloat16)
    up_all, down_all, teach_up_all, teach_down_all = (
        binary_up,
        binary_down,
        teacher_up,
        teacher_down,
    )
    stud_ffn_in, teach_ffn_in = (
        lax.all_gather(stud_normed_low, "mp", axis=0, tiled=True),
        lax.all_gather(teach_normed_low, "mp", axis=0, tiled=True),
    )
    stud_pre, stud_hidden, stud_part = feed_forward(
        stud_ffn_in, up_all, student_up_bias, down_all, clipped_gelu
    )
    teach_pre, teach_hidden, teach_part = feed_forward(
        teach_ffn_in, teach_up_all, teacher_up_bias, teach_down_all, plain_gelu
    )
    stud_branch, teach_branch = (
        lax.psum_scatter(
            stud_part.astype(jnp.bfloat16), "mp", scatter_dimension=0, tiled=True
        ).astype(jnp.float32),
        lax.psum_scatter(
            teach_part.astype(jnp.bfloat16), "mp", scatter_dimension=0, tiled=True
        ).astype(jnp.float32),
    )
    stud_second = stud_normed + stud_branch + stud_out_bias[1]
    teach_second = teach_normed + teach_branch + teach_out_bias[1]
    stud_final = norm_affine(stud_second, stud_gain[1], stud_shift[1])
    teach_final = norm_affine(teach_second, teach_gain[1], teach_shift[1])
    student_output = stud_final.astype(jnp.bfloat16)
    final_grad = token_valid * (stud_final - teach_final)
    unused, stud_back_two = jax.vjp(norm_affine, stud_second, stud_gain[1], stud_shift[1])
    stud_second_grad, gain_two, shift_two = stud_back_two(final_grad)

    def teach_norm_two(values):
        return norm_affine(values, teach_gain[1], teach_shift[1])

    unused, teach_back_two = jax.vjp(teach_norm_two, teach_second)
    teach_second_grad = teach_back_two(-final_grad)[0]
    stud_second_low = stud_second_grad.astype(jnp.bfloat16)
    teach_second_low = teach_second_grad.astype(jnp.bfloat16)
    stud_branch_grad, teach_branch_grad = (
        lax.all_gather(stud_second_low, "mp", axis=0, tiled=True),
        lax.all_gather(teach_second_low, "mp", axis=0, tiled=True),
    )
    stud_pre_grad, stud_pre_low, stud_back_part = feed_back(
        stud_branch_grad, stud_pre, up_all, down_all, clipped_gelu
    )
    teach_pre_grad, teach_pre_low, teach_back_part = feed_back(
        teach_branch_grad, teach_pre, teach_up_all, teach_down_all, plain_gelu
    )
    down_grad = jnp.dot(stud_hidden.T, stud_branch_grad, preferred_element_type=jnp.float32)
    up_grad = jnp.dot(stud_ffn_in.T, stud_pre_low, preferred_element_type=jnp.float32)
    up_bias_grad = jnp.sum(stud_pre_grad, axis=0)
    stud_ffn_back, teach_ffn_back = (
        lax.psum_scatter(
            stud_back_part.astype(jnp.bfloat16), "mp", scatter_dimension=0, tiled=True
        ).astype(jnp.float32),
        lax.psum_scatter(
            teach_back_part.astype(jnp.bfloat16), "mp", scatter_dimension=0, tiled=True
        ).astype(jnp.float32),
    )
    stud_normed_grad = stud_second_grad + stud_ffn_back
    teach_normed_grad = teach_second_grad + teach_ffn_back
    unused, stud_back_one = jax.vjp(norm_affine, stud_first, stud_gain[0], stud_shift[0])
    stud_first_grad, gain_one, shift_one = stud_back_one(stud_normed_grad)

    def teach_norm_one(values):
        return norm_affine(values, teach_gain[0], teach_shift[0])

    unused, teach_back_one = jax.vjp(teach_norm_one, teach_first)
    teach_first_grad = teach_back_one(teach_normed_grad)[0]
    stud_first_low = stud_first_grad.astype(jnp.bfloat16)
    teach_first_low = teach_first_grad.astype(jnp.bfloat16)
    stud_attn_grad, teach_attn_grad = (
        lax.all_gather(stud_first_low, "mp", axis=0, tiled=True),
        lax.all_gather(teach_first_low, "mp", axis=0, tiled=True),
    )
    out_grad = jnp.dot(stud_context.T, stud_attn_grad, preferred_element_type=jnp.float32)
    stud_context_grad = jnp.dot(
        stud_attn_grad, out_all.T, preferred_element_type=jnp.float32
    ).astype(jnp.bfloat16)
    teach_context_grad = jnp.dot(
        teach_attn_grad, teach_out_all.T, preferred_element_type=jnp.float32
    ).astype(jnp.bfloat16)
    stud_scores = raw_scores(stud_query, stud_key, DH)
    teach_scores = raw_scores(teach_query, teach_key, DH)
    score_extra = score_weight * jnp.where(pair_valid, stud_scores - teach_scores, 0.0)
    stud_query_grad, stud_key_grad, stud_value_grad = attend_back(
        stud_query,
        stud_key,
        stud_value,
        stud_lse,
        stud_context_grad,
        stud_scores,
        score_extra,
        key_valid,
        DH,
    )
    teach_query_grad, teach_key_grad, teach_value_grad = attend_back(
        teach_query,
        teach_key,
        teach_value,
        teach_lse,
        teach_context_grad,
        teach_scores,
        -score_extra,
        key_valid,
        DH,
    )
    group_rows = attn_rows.shape[0]
    stud_proj_grad = (
        jnp.stack([stud_query_grad, stud_key_grad, stud_value_grad], axis=1)
        .astype(jnp.bfloat16)
        .reshape(group_rows, 3 * head_cols)
    )
    teach_proj_grad = (
        jnp.stack([teach_query_grad, teach_key_grad, teach_value_grad], axis=1)
        .astype(jnp.bfloat16)
        .reshape(group_rows, 3 * head_cols)
    )
    qkv_grad = jnp.dot(attn_rows.T, stud_proj_grad, preferred_element_type=jnp.float32).reshape(
        features, 3, head_cols
    )
    qv_bias_grad = jnp.stack([jnp.sum(stud_query_grad, axis=0), jnp.sum(stud_value_grad, axis=0)])
    input_part = jnp.dot(
        stud_proj_grad,
        qkv_all.reshape(features, 3 * head_cols).T,
        preferred_element_type=jnp.float32,
    )
    input_part = input_part + jnp.dot(
        teach_proj_grad,
        teach_qkv_all.reshape(features, 3 * head_cols).T,
        preferred_element_type=jnp.float32,
    )
    input_back = lax.psum_scatter(
        input_part.astype(jnp.bfloat16), "mp", scatter_dimension=0, tiled=True
    ).astype(jnp.float32)
    input_grad = input_back + stud_first_grad + teach_first_grad
    out_bias_local = jnp.stack(
        [jnp.sum(stud_first_grad, axis=0), jnp.sum(stud_second_grad, axis=0)]
    )
    gain_local = jnp.stack([gain_one, gain_two])
    shift_local = jnp.stack([shift_one, shift_two])
    out_bias_grad, gain_grad, shift_grad = lax.psum(
        (out_bias_local, gain_local, shift_local), ("dp", "mp")
    )
    qkv_sum, qv_bias_sum, out_sum, up_sum, up_bias_sum, down_sum = (
        lax.psum(qkv_grad.astype(jnp.bfloat16), "dp").astype(jnp.float32),
        lax.psum(qv_bias_grad.astype(jnp.bfloat16), "dp").astype(jnp.float32),
        lax.psum(out_grad.astype(jnp.bfloat16), "dp").astype(jnp.float32),
        lax.psum(up_grad.astype(jnp.bfloat16), "dp").astype(jnp.float32),
        lax.psum(up_bias_grad.astype(jnp.bfloat16), "dp").astype(jnp.float32),
        lax.psum(down_grad.astype(jnp.bfloat16), "dp").astype(jnp.float32),
    )
    return (
        student_output,
        input_grad,
        qkv_sum,
        qv_bias_sum,
        out_sum,
        up_sum,
        up_bias_sum,
        down_sum,
        out_bias_grad,
        gain_grad,
        shift_grad,
    )


def solution(mesh):
    return jax.shard_map(
        per_device,
        mesh=mesh,
        in_specs=(
            P(("dp", "mp"), None),
            P("dp"),
            P(None, None, "mp"),
            P(None, "mp"),
            P("mp", None),
            P(None, "mp"),
            P("mp"),
            P("mp", None),
            P(),
            P(),
            P(),
            P(None, None, "mp"),
            P(None, "mp"),
            P("mp", None),
            P(None, "mp"),
            P("mp"),
            P("mp", None),
            P(),
            P(),
            P(),
        ),
        out_specs=(
            P(("dp", "mp"), None),
            P(("dp", "mp"), None),
            P(None, None, "mp"),
            P(None, "mp"),
            P("mp", None),
            P(None, "mp"),
            P("mp"),
            P("mp", None),
            P(),
            P(),
            P(),
        ),
        check_vma=False,
    )
```

profile of v0, /device:TPU:0, one launch (start us, length us, event | category | flops | bytes accessed | tf_op | source)
XLA Modules:
  0.0 1009.4 jit_solution(6954508182729239959)
XLA Ops:
  9.6 2.3 copy.54
  15.6 42.6 %all-gather.8.cloned.1.call-done = bf16[3072,1024]{1,0:T(8,128)(2,1)} async-done(((bf16[384,1024]{1,0:T(8,128)(2,1)}), bf16[3072,1024]{1,0:T(8,128)(2,1)}) %all-gather.8.cloned.1.call-update) | async-done | bytes 6291472 | tf_op jit(solution)/shard_map/all_gather | solution.py:171
  58.2 5.8 fusion.5
  68.3 2.6 fusion.170
  78.7 3.7 copy.59
  82.5 3.3 copy.55
  96.7 4.5 convolution_convert_fusion.3
  107.0 5.1 convolution_convert_fusion.5
  112.9 50.2 %reduce-scatter.12.cloned.1.call-done = bf16[384,1024]{1,0:T(8,128)(2,1)} async-done(((bf16[3072,1024]{1,0:T(8,128)(2,1)}), bf16[384,1024]{1,0:T(8,128)(2,1)}) %reduce-scatter.12.cloned.1.call-update) | async-done | bytes 786448 | tf_op jit(solution)/shard_map/reduce_scatter | solution.py:188
  163.1 65.6 %reduce-scatter.8.cloned.1.call-done = bf16[384,1024]{1,0:T(8,128)(2,1)} async-done(((bf16[3072,1024]{1,0:T(8,128)(2,1)}), bf16[384,1024]{1,0:T(8,128)(2,1)}) %reduce-scatter.8.cloned.1.call-update) | async-done | bytes 786448 | tf_op jit(solution)/shard_map/reduce_scatter | solution.py:185
  228.7 2.1 fusion.61
  230.8 2.4 multiply_reduce_fusion.9
  236.6 45.0 %all-gather.12.cloned.1.call-done = bf16[3072,1024]{1,0:T(8,128)(2,1)} async-done(((bf16[384,1024]{1,0:T(8,128)(2,1)}), bf16[3072,1024]{1,0:T(8,128)(2,1)}) %all-gather.12.cloned.1.call-update) | async-done | bytes 6291472 | tf_op jit(solution)/shard_map/all_gather | solution.py:206
  281.6 17.9 %fusion.4 = (f32[3072,512]{1,0:T(8,128)S(1)}, f32[3072,512]{1,0:T(8,128)S(1)}) fusion(f32[512]{0:T(512)S(1)} %convert_element_type.275, bf16[3072,1024]{1,0:T(8,128)(2,1)} %all-gather.12.cloned.1.call-done, bf16[1024,512]{1,0:T(8,128)(2,1)} %param.34), kind=kOutput, calls=%fused_computation.7 | convolution fusion | flops 3320315904 | bytes 19924992 | tf_op jit(solution)/shard_map/dot_general | solution.py:109
  299.5 2.7 copy-done.80
  304.0 5.7 convolution_convert_fusion.2
  312.9 16.5 %all-gather.10.cloned.1.call-done = bf16[3072,1024]{1,0:T(8,128)(2,1)} async-done(((bf16[384,1024]{1,0:T(8,128)(2,1)}), bf16[3072,1024]{1,0:T(8,128)(2,1)}) %all-gather.10.cloned.1.call-update) | async-done | bytes 6291472 | tf_op jit(solution)/shard_map/all_gather | solution.py:205
  329.4 21.7 %multiply_convert_fusion.1 = (bf16[3072,512]{1,0:T(8,128)(2,1)S(1)}, f32[3072,512]{1,0:T(8,128)}, f32[3072,512]{1,0:T(8,128)}) fusion(f32[512]{0:T(512)S(1)} %convert_element_type.254, bf16[3072,1024]{1,0:T(8,128)(2,1)} %all-gather.10.cloned.1.call-done, f32[1024,512]{1,0:T(8,128)} %param.25, f32[512]{0:T(512)S(1)} %broadcast_multiply_fusion.1), kind=kOutput, calls=%fused_computation.25 | convolution fusion | flops 3329753088 | bytes 24121344 | tf_op jit(solution)/shard_map/dot_general | solution.py:109
  352.8 5.7 convolution_convert_fusion.4
  359.3 35.1 %reduce-scatter.14.cloned.1.call-done = bf16[384,1024]{1,0:T(8,128)(2,1)} async-done(((bf16[3072,1024]{1,0:T(8,128)(2,1)}), bf16[384,1024]{1,0:T(8,128)(2,1)}) %reduce-scatter.14.cloned.1.call-update) | async-done | bytes 786448 | tf_op jit(solution)/shard_map/reduce_scatter | solution.py:218
  394.4 65.5 %reduce-scatter.10.cloned.1.call-done = bf16[384,1024]{1,0:T(8,128)(2,1)} async-done(((bf16[3072,1024]{1,0:T(8,128)(2,1)}), bf16[384,1024]{1,0:T(8,128)(2,1)}) %reduce-scatter.10.cloned.1.call-update) | async-done | bytes 786448 | tf_op jit(solution)/shard_map/reduce_scatter | solution.py:215
  460.0 2.9 fusion.152
  463.5 2.2 fusion.147
  470.0 2.4 add_convert_fusion.11
  473.0 42.7 %all-gather.18.cloned.1.call-done = bf16[3072,1024]{1,0:T(8,128)(2,1)} async-done(((bf16[384,1024]{1,0:T(8,128)(2,1)}), bf16[3072,1024]{1,0:T(8,128)(2,1)}) %all-gather.18.cloned.1.call-update) | async-done | bytes 6291472 | tf_op jit(solution)/shard_map/all_gather | solution.py:240
  515.7 15.2 %convolution_convert_fusion = bf16[3072,1024]{1,0:T(8,128)(2,1)} fusion(bf16[1024,512]{1,0:T(8,128)(2,1)} %param.34, f32[3072,512]{1,0:T(8,128)} %copy-done.80, f32[3072,512]{1,0:T(8,128)} %copy-done.81, f32[512]{0:T(512)S(1)} %convert_element_type.275, bf16[3072,1024]{1,0:T(8,128)(2,1)} %all-gather.18.cloned.1.call-done, bf16[512,1024]{1,0:T(8,128)(2,1)S(1)} %copy-done), kind=kOutput, calls=%fused_computation.41 | convolution fusion | flops 6469189632 | bytes 27265024 | tf_op jit(solution)/shard_map/dot_general | solution.py:120
  531.0 32.7 %all-gather.14.cloned.1.call-done = bf16[3072,1024]{1,0:T(8,128)(2,1)} async-done(((bf16[384,1024]{1,0:T(8,128)(2,1)}), bf16[3072,1024]{1,0:T(8,128)(2,1)}) %all-gather.14.cloned.1.call-update) | async-done | bytes 6291472 | tf_op jit(solution)/shard_map/all_gather | solution.py:239
  563.7 14.1 %fusion.166 = (bf16[512]{0:T(512)(128)(2,1)S(1)}, bf16[3072,512]{1,0:T(8,128)(2,1)S(1)}) fusion(f32[3072,512]{1,0:T(8,128)} %get-tuple-element.57, bf16[3072,1024]{1,0:T(8,128)(2,1)} %all-gather.14.cloned.1.call-done, f32[512,1024]{1,0:T(8,128)} %param.27, f32[512]{0:T(512)S(1)} %broadcast_multiply_fusion, f32[3072,512]{1,0:T(8,128)} %get-tuple-element.86, ...), kind=kOutput, calls=%fused_computation.264 | convolution fusion | flops 3260546560 | bytes 24122368 | tf_op jit(solution)/shard_map/dot_general | solution.py:116
  579.4 5.6 convolution_convert_fusion.1
  585.1 43.6 %reduce-scatter.18.cloned.1.call-done = bf16[384,1024]{1,0:T(8,128)(2,1)} async-done(((bf16[3072,1024]{1,0:T(8,128)(2,1)}), bf16[384,1024]{1,0:T(8,128)(2,1)}) %reduce-scatter.18.cloned.1.call-update) | async-done | bytes 786448 | tf_op jit(solution)/shard_map/reduce_scatter | solution.py:255
  628.7 65.6 %reduce-scatter.16.cloned.1.call-done = bf16[384,1024]{1,0:T(8,128)(2,1)} async-done(((bf16[3072,1024]{1,0:T(8,128)(2,1)}), bf16[384,1024]{1,0:T(8,128)(2,1)}) %reduce-scatter.16.cloned.1.call-update) | async-done | bytes 786448 | tf_op jit(solution)/shard_map/reduce_scatter | solution.py:252
  694.2 4.3 multiply_reduce_fusion.3
  701.9 2.3 fusion.148
  707.9 8.9 convolution_convert_fusion.8
  716.9 7.3 fusion.49
  724.1 23.3 %all-gather.16.cloned.1.call-done = bf16[3072,1024]{1,0:T(8,128)(2,1)} async-done(((bf16[384,1024]{1,0:T(8,128)(2,1)}), bf16[3072,1024]{1,0:T(8,128)(2,1)}) %all-gather.16.cloned.1.call-update) | async-done | bytes 6291472 | tf_op jit(solution)/shard_map/all_gather | solution.py:272
  747.4 4.7 convolution_convert_fusion.7
  754.8 3.8 fusion.92
  758.6 8.7 multiply_bitcast_fusion
  767.3 3.8 copy.106
  771.8 9.1 fusion.163
  780.9 3.8 copy.105
  786.5 4.1 fusion.162
  790.6 3.7 copy.107
  797.4 2.5 copy.94
  799.9 6.2 convolution_convert_fusion.9
  807.3 4.5 convolution_convert_fusion.13
  812.7 4.6 convolution_convert_fusion.6
  820.2 4.3 fusion.66
  824.6 3.8 copy.110
  829.8 3.5 fusion.86
  833.3 8.0 fusion.70
  841.3 2.2 copy.109
  845.0 8.5 fusion.67
  853.6 4.5 copy.108
  858.1 3.9 reshape.332
  862.0 3.5 fusion.169
  865.5 7.5 fusion.2
  873.1 42.8 %all-reduce = (f32[2,1024]{1,0:T(2,128)}, f32[2,1024]{1,0:T(2,128)}, f32[2,1024]{1,0:T(2,128)}) all-reduce(f32[2,1024]{1,0:T(2,128)S(1)} %pad_maximum_fusion, f32[2,1024]{1,0:T(2,128)S(1)} %pad_maximum_fusion.1, f32[2,1024]{1,0:T(2,128)S(1)} %pad_maximum_fusion.2), channel_id=1, replica_groups=mesh['dp'=4,'mp'=8] {'dp','mp'}, use_global_device_ids=true, to_apply=%region_44.45 | all-reduce | flops 6144 | bytes 49152 | tf_op jit(solution)/shard_map/psum | solution.py:341
  916.1 13.2 %all-reduce.1 = (bf16[2,128]{1,0:T(2,128)(2,1)S(1)}, bf16[512]{0:T(512)(128)(2,1)S(1)}) all-reduce(bf16[2,128]{1,0:T(2,128)(2,1)S(1)} %pad_maximum_fusion.3, bf16[512]{0:T(512)(128)(2,1)S(1)} %get-tuple-element.91), channel_id=1, replica_groups=mesh['dp'=4,'mp'=8] {'dp'}, use_global_device_ids=true, to_apply=%region_36.37 | all-reduce | flops 768 | bytes 3072 | tf_op jit(solution)/shard_map/psum | solution.py:346
  930.5 4.7 all-reduce.5.cloned.1.call-done
  937.1 2.4 convert_element_type.300
  942.7 56.5 %reduce-scatter.20.cloned.1.call-done = bf16[384,1024]{1,0:T(8,128)(2,1)} async-done(((bf16[3072,1024]{1,0:T(8,128)(2,1)}), bf16[384,1024]{1,0:T(8,128)(2,1)}) %reduce-scatter.20.cloned.1.call-update) | async-done | bytes 786448 | tf_op jit(solution)/shard_map/reduce_scatter | solution.py:332
  999.2 3.1 add_add_fusion.4
  (297 shorter events, 82.9 us)
Async XLA Ops:
  7.2 296.9 %copy-start = (bf16[512,1024]{1,0:T(8,128)(2,1)S(1)}, bf16[512,1024]{1,0:T(8,128)(2,1)}, u32[]{:S(2)}) copy-start(bf16[512,1024]{1,0:T(8,128)(2,1)} %param.36) | copy-start | bytes 3145732
  7.2 4.7 copy-start.19
  7.2 51.0 %all-gather.8.cloned.1.call-start = ((), (), s32[]{:S(2)}) async-start(), calls=%async_computation.7 | async-start | bytes 7077888 | tf_op jit(solution)/shard_map/all_gather | solution.py:171
  7.9 155.2 %reduce-scatter.12.cloned.1.call-start = ((), (), s32[]{:S(2)}) async-start(), calls=%async_computation.11 | async-start | bytes 7077888 | tf_op jit(solution)/shard_map/reduce_scatter | solution.py:188
  9.6 4.1 copy-start.75
  13.7 89.6 %copy-start.55 = (pred[24,128]{1,0:T(8,128)(4,1)}, pred[24,128]{1,0:T(8,128)(4,1)S(1)}, u32[]{:S(2)}) copy-start(pred[24,128]{1,0:T(8,128)(4,1)S(1)} %iota_compare_fusion) | copy-start | bytes 9220
  15.6 50.7 %copy-start.25 = (bf16[1024,3,128]{0,2,1:T(8,128)(2,1)}, bf16[1024,3,128]{0,2,1:T(8,128)(2,1)S(1)}, u32[]{:S(2)}) copy-start(bf16[1024,3,128]{0,2,1:T(8,128)(2,1)S(1)} %multiply_convert_fusion.7) | copy-start | bytes 2359300
  64.9 3.4 copy-start.77
  73.8 3.3 copy-start.45
  82.4 7.7 copy-start.32
  101.2 127.5 %reduce-scatter.8.cloned.1.call-start = ((), (), s32[]{:S(2)}) async-start(), calls=%async_computation.8 | async-start | bytes 7077888 | tf_op jit(solution)/shard_map/reduce_scatter | solution.py:185
  102.3 3.8 copy-start.71
  112.1 116.5 %copy-start.2 = (bf16[384,1024]{1,0:T(8,128)(2,1)S(1)}, bf16[384,1024]{1,0:T(8,128)(2,1)}, u32[]{:S(2)}) copy-start(bf16[384,1024]{1,0:T(8,128)(2,1)} %param.20) | copy-start | bytes 2359300
  112.2 169.4 %all-gather.12.cloned.1.call-start = ((), (), s32[]{:S(2)}) async-start(), calls=%async_computation.12 | async-start | bytes 7077888 | tf_op jit(solution)/shard_map/all_gather | solution.py:206
  163.1 70.7 %copy-start.5 = (bf16[384,1024]{1,0:T(8,128)(2,1)S(1)}, bf16[384,1024]{1,0:T(8,128)(2,1)}, u32[]{:S(2)}) copy-start(bf16[384,1024]{1,0:T(8,128)(2,1)} %reduce-scatter.12.cloned.1.call-done) | copy-start | bytes 2359300
  228.7 5.1 copy-start.6
  233.2 3.3 copy-start.73
  235.9 93.5 %all-gather.10.cloned.1.call-start = ((), (), s32[]{:S(2)}) async-start(), calls=%async_computation.9 | async-start | bytes 7077888 | tf_op jit(solution)/shard_map/all_gather | solution.py:205
  236.5 157.9 %reduce-scatter.14.cloned.1.call-start = ((), (), s32[]{:S(2)}) async-start(), calls=%async_computation.13 | async-start | bytes 7077888 | tf_op jit(solution)/shard_map/reduce_scatter | solution.py:218
  299.5 4.6 copy-start.81
  309.8 150.2 %reduce-scatter.10.cloned.1.call-start = ((), (), s32[]{:S(2)}) async-start(), calls=%async_computation.10 | async-start | bytes 7077888 | tf_op jit(solution)/shard_map/reduce_scatter | solution.py:215
  329.4 23.3 %copy-start.47 = (f32[512,1024]{1,0:T(8,128)S(1)}, f32[512,1024]{1,0:T(8,128)}, u32[]{:S(2)}) copy-start(f32[512,1024]{1,0:T(8,128)} %param.27) | copy-start | bytes 6291460
  358.5 157.1 %all-gather.18.cloned.1.call-start = ((), (), s32[]{:S(2)}) async-start(), calls=%async_computation.17 | async-start | bytes 7077888 | tf_op jit(solution)/shard_map/all_gather | solution.py:240
  470.0 93.7 %all-gather.14.cloned.1.call-start = ((), (), s32[]{:S(2)}) async-start(), calls=%async_computation.14 | async-start | bytes 7077888 | tf_op jit(solution)/shard_map/all_gather | solution.py:239
  472.5 156.2 %reduce-scatter.18.cloned.1.call-start = ((), (), s32[]{:S(2)}) async-start(), calls=%async_computation.18 | async-start | bytes 7077888 | tf_op jit(solution)/shard_map/reduce_scatter | solution.py:255
  530.9 163.3 %reduce-scatter.16.cloned.1.call-start = ((), (), s32[]{:S(2)}) async-start(), calls=%async_computation.15 | async-start | bytes 7077888 | tf_op jit(solution)/shard_map/reduce_scatter | solution.py:252
  563.7 15.7 %copy-start.48 = (f32[1024,512]{1,0:T(8,128)S(1)}, f32[1024,512]{1,0:T(8,128)}, u32[]{:S(2)}) copy-start(f32[1024,512]{1,0:T(8,128)} %param.25) | copy-start | bytes 6291460
  585.0 113.5 %copy-start.64 = (f32[384]{0:T(512)S(1)}, f32[384]{0:T(512)}, u32[]{:S(2)}) copy-start(f32[384]{0:T(512)} %copy-done.63) | copy-start | bytes 4612
  585.0 162.4 %all-gather.16.cloned.1.call-start = ((), (), s32[]{:S(2)}) async-start(), calls=%async_computation.16 | async-start | bytes 7077888 | tf_op jit(solution)/shard_map/all_gather | solution.py:272
  694.2 4.3 copy-start.8
  694.2 4.3 copy-start.29
  698.5 3.3 copy-start.62
  698.5 3.3 copy-start.28
  701.8 110.1 %all-gather.20.cloned.1.call-start = ((), (), s32[]{:S(2)}) async-start(), calls=%async_computation.19 | async-start | bytes 7077888 | tf_op jit(solution)/shard_map/all_gather | solution.py:273
  701.8 4.6 copy-start.56
  706.4 228.8 %all-reduce.5.cloned.1.call-start = ((), (), s32[]{:S(2)}) async-start(), calls=%async_computation.21 | async-start | bytes 6291456 | tf_op jit(solution)/shard_map/psum | solution.py:345
  707.9 8.9 copy-start.79
  716.8 30.6 %copy-start.23 = (f32[128,1024]{1,0:T(8,128)S(1)}, f32[128,1024]{1,0:T(8,128)}, u32[]{:S(2)}) copy-start(f32[128,1024]{1,0:T(8,128)} %param.24) | copy-start | bytes 1572868
  716.8 30.6 %copy-start.72 = (f32[128]{0:T(128)S(1)}, f32[128]{0:T(128)}, u32[]{:S(2)}) copy-start(f32[128]{0:T(128)} %copy-done.71) | copy-start | bytes 1540
  752.8 5.8 copy-start.39
  752.8 5.8 copy-start.60
  754.8 3.8 copy-start.41
  754.8 3.8 copy-start.51
  767.3 4.5 copy-start.31
  771.8 24.0 %copy-start.15 = (bf16[3072,1,128]{2,0,1:T(8,128)(2,1)}, bf16[3072,1,128]{2,0,1:T(8,128)(2,1)S(1)}, u32[]{:S(2)}) copy-start(bf16[3072,1,128]{2,0,1:T(8,128)(2,1)S(1)} %reshape.330) | copy-start | bytes 2359300
  780.9 5.6 copy-start.42
  799.9 7.3 copy-start.14
  811.8 187.4 %reduce-scatter.20.cloned.1.call-start = ((), (), s32[]{:S(2)}) async-start(), calls=%async_computation.20 | async-start | bytes 7077888 | tf_op jit(solution)/shard_map/reduce_scatter | solution.py:332
  817.3 2.9 copy-start.58
  820.2 4.3 copy-start.44
  824.6 5.3 copy-start.37
  828.3 5.0 copy-start.35
  829.8 3.5 copy-start.52
  841.3 3.7 copy-start.33
  853.5 8.4 copy-start.16
  853.5 8.4 copy-start.17
  853.5 8.4 copy-start.18
  853.6 8.4 copy-start.26
  862.0 3.5 copy-start.24
  862.0 3.5 copy-start.27
  935.2 4.3 copy-start.50
  935.2 5.9 copy-start.49
  939.5 59.7 %copy-start.10 = (f32[384,1024]{1,0:T(8,128)S(1)}, f32[384,1024]{1,0:T(8,128)}, u32[]{:S(2)}) copy-start(f32[384,1024]{1,0:T(8,128)} %copy-done.9) | copy-start | bytes 4718596
  941.1 61.2 %copy-start.1 = (bf16[512,1024]{1,0:T(8,128)(2,1)S(1)}, bf16[512,1024]{1,0:T(8,128)(2,1)}, u32[]{:S(2)}) copy-start(bf16[512,1024]{1,0:T(8,128)(2,1)} %param.36) | copy-start | bytes 3145732
  (34 other events, 45.8 us)
Sparse Core Ops, SparseCore 0:
  9.9 48.2 all-gather.7
  101.3 61.7 reduce-scatter.11
  166.9 61.7 reduce-scatter.7
  236.0 45.4 all-gather.11
  283.9 45.5 all-gather.9
  332.7 61.7 reduce-scatter.13
  398.2 61.7 reduce-scatter.9
  470.1 45.5 all-gather.17
  518.1 45.5 all-gather.13
  566.9 61.7 reduce-scatter.17
  632.4 61.7 reduce-scatter.15
  701.9 45.4 all-gather.15
  749.3 45.5 all-gather.19
  811.9 123.2 all-reduce.4
  938.4 60.7 reduce-scatter.19
where the time goes:
time: 1020 us; the launch traced here: 1010 us
  waiting for transfers between devices  591 us (58%)
  matrix products  206 us (20%)
  local copies, waits for them, and re-layouts  87.9 us (9%)
  blocking collectives  56 us (5%)
  other arithmetic  51.1 us (5%)
  between operations  15.5 us (2%)
    reduce_scatter x1, waiting for transfers between devices, per_device(): lax.psum_scatter(stud_back_part.astype(jnp.bfloat16), 'mp', scatter_dimen...  65.6 us
    reduce_scatter x1, waiting for transfers between devices, per_device(): lax.psum_scatter(stud_attn_part.astype(jnp.bfloat16), 'mp', scatter_dimen...  65.6 us
    reduce_scatter x1, waiting for transfers between devices, per_device(): lax.psum_scatter(stud_part.astype(jnp.bfloat16), 'mp', scatter_dimension=...  65.5 us
    reduce_scatter x1, waiting for transfers between devices, per_device(): lax.psum_scatter(input_part.astype(jnp.bfloat16), 'mp', scatter_dimension...  56.5 us
    reduce_scatter x1, waiting for transfers between devices, per_device(): lax.psum_scatter(teach_attn_part.astype(jnp.bfloat16), 'mp', scatter_dime...  50.2 us
    all_gather x1, waiting for transfers between devices, per_device(): lax.all_gather(teach_normed_low, 'mp', axis=0, tiled=True)  45 us
    reduce_scatter x1, waiting for transfers between devices, per_device(): lax.psum_scatter(teach_back_part.astype(jnp.bfloat16), 'mp', scatter_dime...  43.6 us
    psum x1, blocking collectives, per_device(): lax.psum((out_bias_local, gain_local, shift_local), ('dp', 'mp'))  42.8 us
  transfers between devices with their start and end apart: 15, of which 14 were waited for; matrix products, arithmetic and copies ran while one was open for 26% of the time, Pallas kernels for 0%

commit v1 on v0

v1 whole, which is shorter than its diff:
```python
import math

import jax
import jax.numpy as jnp
from jax import lax
from jax.experimental import pallas as pl
from jax.experimental.pallas import tpu as pltpu
from jax.sharding import PartitionSpec as P

DH = 64
LEN = 128


norm_epsilon = 1e-06
clip_level = 2.5
score_weight = 0.05
masked_fill = -1000000000.0


def to_float(values):
    return values.astype(jnp.float32)


def to_low(values):
    return values.astype(jnp.bfloat16)


def binarize(matrix, axis_index):
    scaling = jnp.mean(jnp.abs(matrix), axis=axis_index, keepdims=True)
    return (scaling * jnp.sign(matrix)).astype(jnp.bfloat16)


def norm_stats(values):
    centred = values - jnp.mean(values, axis=-1, keepdims=True)
    variance = jnp.mean(centred * centred, axis=-1, keepdims=True)
    inverse = lax.rsqrt(variance + norm_epsilon)
    return (centred * inverse, inverse)


def norm_back(grad, unit, inverse, gain_row):
    scaled = grad * gain_row
    first = jnp.mean(scaled, axis=-1, keepdims=True)
    second = jnp.mean(scaled * unit, axis=-1, keepdims=True)
    return inverse * (scaled - first - unit * second)


def dot(left, right):
    return jnp.dot(left, right, preferred_element_type=jnp.float32)


def dot_nt(left, right):
    return lax.dot_general(left, right, (((1,), (1,)), ((), ())), preferred_element_type=jnp.float32)


def dot_tn(left, right):
    return lax.dot_general(left, right, (((0,), (0,)), ((), ())), preferred_element_type=jnp.float32)


class Cube:
    def __init__(self, n_dp):
        self.n_dp = n_dp
        self.axes = ("dp", "mp")

    def flip(self, values, bits):
        pairs = [
            (z * 8 + m, z * 8 + (m ^ bits)) for z in range(self.n_dp) for m in range(8)
        ]
        return lax.ppermute(values, self.axes, pairs)

    def flip_dp(self, values, bits):
        pairs = [
            (z * 8 + m, (z ^ bits) * 8 + m) for z in range(self.n_dp) for m in range(8)
        ]
        return lax.ppermute(values, self.axes, pairs)

    def gather(self, block):
        half = block.shape[0] // 2
        along_x = self.flip(block, 2)
        along_y = self.flip(block, 4)
        across = jnp.concatenate(
            [self.flip(along_y[:half], 2), self.flip(along_x[half:], 4)], axis=0
        )
        same = [block, along_x, along_y, across]
        other = [self.flip(item, 1) for item in same]
        return [item for pair in zip(same, other) for item in pair]

    def scatter(self, blocks):
        half = blocks[0].shape[0] // 2
        own, to_x, to_y, to_far = [
            to_float(blocks[k]) + to_float(self.flip(blocks[k + 1], 1)) for k in (0, 2, 4, 6)
        ]
        far = to_low(to_far)
        via_x = to_float(self.flip(far[:half], 2))
        via_y = to_float(self.flip(far[half:], 4))
        to_y = to_low(jnp.concatenate([to_y[:half] + via_x, to_y[half:]], axis=0))
        to_x = to_low(jnp.concatenate([to_x[:half], to_x[half:] + via_y], axis=0))
        return own + to_float(self.flip(to_x, 2)) + to_float(self.flip(to_y, 4))

    def sum_dp(self, values):
        half = values.shape[0] // 2
        odd = lax.axis_index("dp") % 2
        low = to_low(values)
        sent = lax.dynamic_slice_in_dim(low, (1 - odd) * half, half)
        kept = lax.dynamic_slice_in_dim(values, odd * half, half)
        kept = kept + to_float(self.flip_dp(sent, 1))
        kept_low = to_low(kept)
        kept = to_low(kept + to_float(self.flip_dp(kept_low, 2)))
        other = self.flip_dp(kept, 1)
        return to_float(
            jnp.concatenate(
                [jnp.where(odd == 0, kept, other), jnp.where(odd == 0, other, kept)], axis=0
            )
        )

    def sum_all(self, values):
        for bits in (1, 2, 4):
            values = values + self.flip(values, bits)
        for bits in (1, 2):
            values = values + self.flip_dp(values, bits)
        return values

    def place(self, values):
        me = lax.axis_index("mp")
        for bit in range(3):
            shape = values.shape
            split = values.reshape((8 >> (bit + 1), 2, 1 << bit) + shape[1:])
            flipped = split[:, ::-1]
            values = jnp.where((me >> bit) % 2 == 1, flipped, split).reshape(shape)
        return values


class Plain:
    def __init__(self, n_mp):
        self.n_mp = n_mp

    def gather(self, block):
        every = lax.all_gather(block, "mp", axis=0)
        return [every[k] for k in range(self.n_mp)]

    def scatter(self, blocks):
        return to_float(
            lax.psum_scatter(jnp.stack(blocks), "mp", scatter_dimension=0, tiled=False)
        )

    def sum_dp(self, values):
        return to_float(lax.psum(to_low(values), "dp"))

    def sum_all(self, values):
        return lax.psum(values, ("dp", "mp"))

    def place(self, values):
        return values


def plain_act(pre):
    gate = 0.5 * (1.0 + lax.erf(pre * math.sqrt(0.5)))
    slope = gate + pre * jnp.exp(-0.5 * pre * pre) * (1.0 / math.sqrt(2.0 * math.pi))
    return (pre * gate, slope)


def clipped_act(pre):
    value, slope = plain_act(pre)
    bent = jnp.tanh(value * (1.0 / clip_level))
    return (clip_level * bent, slope * (1.0 - bent * bent))


def gather_layer(net, qkv, qv_bias, out, up, up_bias, down):
    width = qkv.shape[2]
    units = up.shape[1]
    features = qkv.shape[0]
    extra = jnp.zeros((16, features), jnp.bfloat16)
    extra = extra.at[0, :width].set(qv_bias[0]).at[1, :width].set(qv_bias[1])
    extra = extra.at[2, :units].set(up_bias)
    qkv_parts = net.gather(qkv.transpose(1, 0, 2).reshape(3 * features, width))
    out_parts = net.gather(jnp.concatenate([out, extra], axis=0))
    up_parts = net.gather(up)
    down_parts = net.gather(down)
    count = len(qkv_parts)
    qkv_full = jnp.concatenate(
        [part.reshape(3, features, width) for part in qkv_parts], axis=2
    )
    out_full = jnp.concatenate([part[:width] for part in out_parts], axis=0)
    q_bias = jnp.concatenate([part[width, :width] for part in out_parts])
    v_bias = jnp.concatenate([part[width + 1, :width] for part in out_parts])
    up_b = jnp.concatenate([part[width + 2, :units] for part in out_parts])
    up_full = jnp.concatenate(up_parts, axis=1)
    down_full = jnp.concatenate(down_parts, axis=0)
    return (qkv_full, to_float(q_bias), to_float(v_bias), out_full, up_full, to_float(up_b), down_full)


def forward(tokens, weights, out_bias, gain, shift, activation, key_valid):
    qkv, q_bias, v_bias, out, up, up_bias, down = weights
    rows, features = tokens.shape
    pairs = rows // LEN
    shape = (pairs, LEN, features // DH, DH)
    query = to_low(dot(tokens, qkv[0]) + q_bias).reshape(shape)
    key = to_low(dot(tokens, qkv[1])).reshape(shape)
    value = to_low(dot(tokens, qkv[2]) + v_bias).reshape(shape)
    scores = jnp.einsum("bqhe,bkhe->bhqk", query, key, preferred_element_type=jnp.float32) * (
        1.0 / math.sqrt(DH)
    )
    masked = jnp.where(key_valid[:, None, None, :], scores, masked_fill)
    log_norm = jax.nn.logsumexp(masked, axis=-1, keepdims=True)
    attention = jnp.exp(masked - log_norm)
    context = jnp.einsum(
        "bhqk,bkhe->bqhe", to_low(attention), value, preferred_element_type=jnp.float32
    )
    context = to_low(context).reshape(rows, features)
    first = to_float(tokens) + dot(context, out) + out_bias[0]
    unit_one, inverse_one = norm_stats(first)
    normed = unit_one * gain[0] + shift[0]
    normed_low = to_low(normed)
    hidden, slope = activation(dot(normed_low, up) + up_bias)
    hidden = to_low(hidden)
    second = normed + dot(hidden, down) + out_bias[1]
    unit_two, inverse_two = norm_stats(second)
    final = unit_two * gain[1] + shift[1]
    kept = (query, key, value, scores, attention, context, unit_one, inverse_one, normed_low, hidden,
            to_low(slope), unit_two, inverse_two)
    return (final, kept)


def backward_ffn(kept, weights, second_grad, gain):
    qkv, q_bias, v_bias, out, up, up_bias, down = weights
    (query, key, value, scores, attention, context, unit_one, inverse_one, normed_low, hidden,
     slope, unit_two, inverse_two) = kept
    second_low = to_low(second_grad)
    pre_grad = dot_nt(second_low, down) * slope
    pre_low = to_low(pre_grad)
    normed_grad = second_grad + dot_nt(pre_low, up)
    first_grad = norm_back(normed_grad, unit_one, inverse_one, gain[0])
    return (second_grad, second_low, pre_grad, pre_low, normed_grad, first_grad)


def backward_attention(kept, first_low, out, extra):
    query, key, value, scores, attention = kept[:5]
    rows = first_low.shape[0]
    factor = 1.0 / math.sqrt(DH)
    context_grad = to_low(dot_nt(first_low, out)).reshape(query.shape)
    attention_grad = jnp.einsum(
        "bqhe,bkhe->bhqk", context_grad, value, preferred_element_type=jnp.float32
    )
    value_grad = jnp.einsum(
        "bhqk,bqhe->bkhe", to_low(attention), context_grad, preferred_element_type=jnp.float32
    )
    inner = jnp.sum(attention * attention_grad, axis=-1, keepdims=True)
    score_low = to_low(attention * (attention_grad - inner) + extra)
    query_grad = factor * jnp.einsum(
        "bhqk,bkhe->bqhe", score_low, key, preferred_element_type=jnp.float32
    )
    key_grad = factor * jnp.einsum(
        "bhqk,bqhe->bkhe", score_low, query, preferred_element_type=jnp.float32
    )
    return [item.reshape(rows, -1) for item in (query_grad, key_grad, value_grad)]


MESH = pl.DeviceIdType.MESH
SLOTS = 8
PACKS = 6
ATT_ROWS = 528
FFN_ROWS = 512
HALF_UNITS = 256
COLS = 128


def flipped(me, bits):
    return me + bits - 2 * bits * lax.rem(lax.div(me, bits), 2)


def pack_rows(pack):
    return ATT_ROWS if pack < 2 else FFN_ROWS


def pack_half(pack):
    return 272 if pack < 2 else 256


def masked_probs(scores, length):
    rows = scores.shape[0]
    position = lax.broadcasted_iota(jnp.int32, (rows, LEN), 1)
    parts = []
    for head in range(2):
        part = jnp.where(position < length, scores[:, head * LEN : (head + 1) * LEN], masked_fill)
        part = jnp.exp(part - jnp.max(part, axis=1, keepdims=True))
        parts.append(part / jnp.sum(part, axis=1, keepdims=True))
    return jnp.concatenate(parts, axis=1)


def two_heads(rows):
    first = lax.broadcasted_iota(jnp.int32, rows.shape, 1) < DH
    zero = jnp.zeros_like(rows)
    return jnp.concatenate([jnp.where(first, rows, zero), jnp.where(first, zero, rows)], axis=0)


def norm_block(values):
    centred = values - jnp.mean(values, axis=1, keepdims=True)
    inverse = lax.rsqrt(jnp.mean(centred * centred, axis=1, keepdims=True) + norm_epsilon)
    return (centred * inverse, inverse)


def forward_kernel(
    lengths,
    x_ref,
    packs_att,
    packs_ffn,
    t_bias,
    t_gain,
    t_shift,
    s_bias,
    s_gain,
    s_shift,
    gathered,
    qkv_t,
    qkv_s,
    context_s,
    slope_t,
    slope_s,
    hidden_s,
    unit_t,
    inverse_t,
    unit_s,
    inverse_s,
    low_s,
    grad_t,
    grad_s,
    final_low,
    vectors,
    wide,
    total,
    normed,
    low_t,
    context_t,
    bias_rows,
    final_t,
    unit_two,
    inverse_two,
    send,
    recv,
    load,
    own,
):
    me = lax.axis_index("mp")
    peers = {1: flipped(me, 1), 2: flipped(me, 2), 4: flipped(me, 4)}
    rows = x_ref.shape[0]
    pairs = rows // LEN

    barrier = pltpu.get_barrier_semaphore()
    for peer in peers.values():
        pl.semaphore_signal(barrier, inc=1, device_id={"mp": peer}, device_id_type=MESH)
    pl.semaphore_wait(barrier, 3)

    def source(pack):
        return packs_att.at[pack] if pack < 2 else packs_ffn.at[pack - 2]

    def block(pack, slot, start=0, count=None):
        count = pack_rows(pack) if count is None else count
        return gathered.at[pack, slot, pl.ds(start, count)]

    def remote(pack, kind):
        half = pack_half(pack)
        rest = pack_rows(pack) - half
        if kind == 0:
            src, dst, bits = source(pack), block(pack, 2), 2
        elif kind == 1:
            src, dst, bits = source(pack), block(pack, 4), 4
        elif kind == 2:
            src, dst, bits = block(pack, 4, 0, half), block(pack, 6, 0, half), 2
        elif kind == 3:
            src, dst, bits = block(pack, 2, half, rest), block(pack, 6, half, rest), 4
        elif kind == 4:
            src, dst, bits = source(pack), block(pack, 1), 1
        else:
            slot = 2 * (kind - 4)
            src, dst, bits = block(pack, slot), block(pack, slot + 1), 1
        return pltpu.make_async_remote_copy(
            src_ref=src,
            dst_ref=dst,
            send_sem=send.at[pack, kind],
            recv_sem=recv.at[pack, kind],
            device_id={"mp": peers[bits]},
            device_id_type=MESH,
        )

    def keep_own(pack):
        return pltpu.make_async_copy(source(pack), block(pack, 0), own.at[pack])

    def first_sends(pack):
        for kind in (0, 1, 4):
            remote(pack, kind).start()
        keep_own(pack).start()

    def second_sends(pack):
        remote(pack, 0).wait_recv()
        remote(pack, 3).start()
        remote(pack, 5).start()
        remote(pack, 1).wait_recv()
        remote(pack, 2).start()
        remote(pack, 6).start()

    def load_pair(pack, pair, place):
        return pltpu.make_async_copy(
            gathered.at[pack, pl.ds(2 * pair, 2), pl.ds(0, pack_rows(pack))],
            wide.at[place, :, pl.ds(0, pack_rows(pack))],
            load.at[place],
        )

    def over_pairs(pack, body):
        keep_own(pack).wait()
        remote(pack, 4).wait_recv()
        load_pair(pack, 0, 0).start()
        for pair in range(4):
            place = pair % 2
            load_pair(pack, pair, place).wait()
            if pair < 3:
                if pair == 2:
                    remote(pack, 2).wait_recv()
                    remote(pack, 3).wait_recv()
                    remote(pack, 7).start()
                remote(pack, 5 + pair).wait_recv()
                load_pair(pack, pair + 1, 1 - place).start()
            body(pair, place)

    def attention(pack, qkv_ref, context_ref):
        total[...] = jnp.zeros_like(total)

        def body(pair, place):
            weights = wide[place, :, 0:384].reshape(768, -1)
            projected = dot_nt(x_ref[...], weights)
            for side in range(2):
                slot = 2 * pair + side
                bias = wide[place, side, 512:528]
                bias_rows[pack, slot] = bias
                bias = to_float(bias[0:1])
                part = projected[:, side * 384 : side * 384 + 384]
                query = to_low(part[:, :COLS] + bias[:, :COLS])
                key = to_low(part[:, COLS : 2 * COLS])
                value = to_low(part[:, 2 * COLS :] + bias[:, COLS : 2 * COLS])
                qkv_ref[slot, :, 0:COLS] = query
                qkv_ref[slot, :, COLS : 2 * COLS] = key
                qkv_ref[slot, :, 2 * COLS : 3 * COLS] = value
                for number in range(pairs):
                    here = slice(number * LEN, (number + 1) * LEN)
                    scores = dot_nt(query[here], two_heads(key[here])) * (1.0 / math.sqrt(DH))
                    probs = masked_probs(scores, lengths[me * pairs + number])
                    part_context = dot(to_low(probs), two_heads(value[here]))
                    context_ref[pair, here, side * COLS : (side + 1) * COLS] = to_low(part_context)
            total[...] += dot(context_ref[pair], wide[place, :, 384:512].reshape(256, -1))

        over_pairs(pack, body)

    def first_norm(bias_ref, gain_ref, shift_ref, unit_ref, inverse_ref, index, low_ref):
        @pl.loop(0, rows // 64)
        def _(step):
            here = pl.ds(step * 64, 64)
            values = to_float(x_ref[here]) + total[here] + to_float(bias_ref[0:1])
            unit, inverse = norm_block(values)
            unit_ref[here] = unit
            inverse_ref[here] = inverse
            values = unit * to_float(gain_ref[0:1]) + to_float(shift_ref[0:1])
            normed[index, here] = values
            low_ref[here] = to_low(values)

    def feed_forward(layer, half, low_ref, activation, hidden_ref, slope_ref):
        pack = 2 + 2 * layer + half

        def body(pair, place):
            up = wide[place, :, 0:HALF_UNITS].reshape(2 * HALF_UNITS, -1)
            down = wide[place, :, HALF_UNITS : 2 * HALF_UNITS].reshape(2 * HALF_UNITS, -1)
            start = 2 * COLS + half * HALF_UNITS
            bias = jnp.concatenate(
                [
                    to_float(bias_rows[layer, 2 * pair + side, 0:1, start : start + HALF_UNITS])
                    for side in range(2)
                ],
                axis=1,
            )
            hidden, slope = activation(dot_nt(low_ref[...], up) + bias)
            hidden = to_low(hidden)
            slope_ref[half, pair] = to_low(slope)
            if hidden_ref is not None:
                hidden_ref[half, pair] = hidden
            total[...] += dot(hidden, down)

        if half == 0:
            total[...] = jnp.zeros_like(total)
        over_pairs(pack, body)

    def step_teacher_end():
        @pl.loop(0, rows // 64)
        def _(step):
            here = pl.ds(step * 64, 64)
            unit, inverse = norm_block(normed[0, here] + total[here] + to_float(t_bias[1:2]))
            unit_two[here] = unit
            inverse_two[here] = inverse
            final_t[here] = unit * to_float(t_gain[1:2]) + to_float(t_shift[1:2])

    def step_student_end():
        vectors[...] = jnp.zeros_like(vectors)

        @pl.loop(0, rows // 64)
        def _(step):
            here = pl.ds(step * 64, 64)
            unit, inverse = norm_block(normed[1, here] + total[here] + to_float(s_bias[1:2]))
            gain = to_float(s_gain[1:2])
            final = unit * gain + to_float(s_shift[1:2])
            final_low[here] = to_low(final)
            position = lax.broadcasted_iota(jnp.int32, (64, 1), 0) + lax.rem(step, 2) * 64
            valid = position < lengths[me * pairs + lax.div(step, 2)]
            grad = jnp.where(valid, final - final_t[here], 0.0)
            back = norm_back(grad, unit, inverse, gain)
            grad_s[here] = back
            grad_t[here] = norm_back(
                -grad, unit_two[here], inverse_two[here], to_float(t_gain[1:2])
            )
            vectors[0:1] += jnp.sum(back, axis=0, keepdims=True)
            vectors[1:2] += jnp.sum(grad * unit, axis=0, keepdims=True)
            vectors[2:3] += jnp.sum(grad, axis=0, keepdims=True)

    def use(pack):
        if pack == 0:
            attention(0, qkv_t, context_t)
            first_norm(t_bias, t_gain, t_shift, unit_t, inverse_t, 0, low_t)
        elif pack == 1:
            attention(1, qkv_s, context_s)
            first_norm(s_bias, s_gain, s_shift, unit_s, inverse_s, 1, low_s)
        elif pack < 4:
            feed_forward(0, pack - 2, low_t, plain_act, None, slope_t)
            if pack == 3:
                step_teacher_end()
        else:
            feed_forward(1, pack - 4, low_s, clipped_act, hidden_s, slope_s)
            if pack == 5:
                step_student_end()

    first_sends(0)
    first_sends(1)
    for pack in range(PACKS):
        second_sends(pack)
        if pack + 2 < PACKS:
            first_sends(pack + 2)
        if pack:
            use(pack - 1)
    use(PACKS - 1)
    for pack in range(PACKS):
        for kind in range(8):
            remote(pack, kind).wait_send()


def forward_both(lengths, tokens, packs_att, packs_ffn, teacher_rows, student_rows):
    rows, features = tokens.shape
    low, full = jnp.bfloat16, jnp.float32
    vmem = pl.BlockSpec(memory_space=pltpu.VMEM)
    hbm = pl.BlockSpec(memory_space=pl.ANY)
    shapes = [
        ((PACKS, SLOTS, ATT_ROWS, features), low, hbm),
        ((SLOTS, rows, 3 * COLS), low, vmem),
        ((SLOTS, rows, 3 * COLS), low, vmem),
        ((4, rows, 2 * COLS), low, vmem),
        ((2, 4, rows, 2 * HALF_UNITS), low, vmem),
        ((2, 4, rows, 2 * HALF_UNITS), low, vmem),
        ((2, 4, rows, 2 * HALF_UNITS), low, vmem),
        ((rows, features), full, vmem),
        ((rows, 1), full, vmem),
        ((rows, features), full, vmem),
        ((rows, 1), full, vmem),
        ((rows, features), low, vmem),
        ((rows, features), full, vmem),
        ((rows, features), full, vmem),
        ((rows, features), low, vmem),
        ((8, features), full, vmem),
    ]
    return pl.pallas_call(
        forward_kernel,
        out_shape=[jax.ShapeDtypeStruct(shape, kind) for shape, kind, _ in shapes],
        in_specs=[pl.BlockSpec(memory_space=pltpu.SMEM), vmem, hbm, hbm] + [vmem] * 6,
        out_specs=[spec for _, _, spec in shapes],
        scratch_shapes=[
            pltpu.VMEM((2, 2, ATT_ROWS, features), low),
            pltpu.VMEM((rows, features), full),
            pltpu.VMEM((2, rows, features), full),
            pltpu.VMEM((rows, features), low),
            pltpu.VMEM((4, rows, 2 * COLS), low),
            pltpu.VMEM((2, SLOTS, 16, features), low),
            pltpu.VMEM((rows, features), full),
            pltpu.VMEM((rows, features), full),
            pltpu.VMEM((rows, 1), full),
            pltpu.SemaphoreType.DMA((PACKS, 8)),
            pltpu.SemaphoreType.DMA((PACKS, 8)),
            pltpu.SemaphoreType.DMA((2,)),
            pltpu.SemaphoreType.DMA((PACKS,)),
        ],
        compiler_params=pltpu.CompilerParams(
            collective_id=0, has_side_effects=True, vmem_limit_bytes=60 * 1024 * 1024
        ),
        name="forward_both",
    )(lengths, tokens, packs_att, packs_ffn, *teacher_rows, *student_rows)


def pack_layer(qkv, qv_bias, out, up, up_bias, down):
    features, _, width = qkv.shape
    bias = jnp.concatenate([qv_bias.reshape(-1), up_bias])
    bias = jnp.pad(bias[None], ((0, 15), (0, features - bias.size)))
    att = jnp.concatenate([qkv.transpose(1, 2, 0).reshape(3 * width, features), out, bias], axis=0)
    halves = [
        jnp.concatenate(
            [
                up[:, h * HALF_UNITS : (h + 1) * HALF_UNITS].T,
                down[h * HALF_UNITS : (h + 1) * HALF_UNITS],
            ],
            axis=0,
        )
        for h in range(2)
    ]
    return (att, jnp.stack(halves))


def cut(values, count, axis):
    return jnp.split(values, count, axis=axis)


def per_device(n_dp, n_mp, *args):
    (
        tokens,
        lengths,
        student_qkv,
        student_qv_bias,
        student_out,
        student_up,
        student_up_bias,
        student_down,
        student_out_bias,
        student_gain,
        student_shift,
        teacher_qkv,
        teacher_qv_bias,
        teacher_out,
        teacher_up,
        teacher_up_bias,
        teacher_down,
        teacher_out_bias,
        teacher_gain,
        teacher_shift,
    ) = args
    net = Cube(n_dp) if (n_dp, n_mp) == (4, 8) else Plain(n_mp)
    rows = tokens.shape[0]
    pairs = rows // LEN
    places = jnp.arange(LEN, dtype=jnp.int32)
    me = lax.axis_index("mp")
    own_lengths = lax.dynamic_slice_in_dim(lengths, me * pairs, pairs)
    valid = places[None, :] < own_lengths[:, None]
    token_valid = to_float(valid.reshape(rows, 1))
    pair_valid = valid[:, None, :, None] & valid[:, None, None, :]

    gain = to_float(student_gain)
    shift = to_float(student_shift)
    out_bias = to_float(student_out_bias)
    teach_gain = to_float(teacher_gain)
    if isinstance(net, Cube):
        teach_att, teach_ffn = pack_layer(
            teacher_qkv, teacher_qv_bias, teacher_out, teacher_up, teacher_up_bias, teacher_down
        )
        stud_att, stud_ffn = pack_layer(
            binarize(student_qkv, 0),
            student_qv_bias,
            binarize(student_out, 1),
            binarize(student_up, 0),
            student_up_bias,
            binarize(student_down, 1),
        )
        (gathered, qkv_t, qkv_s, context_s, slope_t, slope_s, hidden_s, unit_t, inverse_t, unit_s,
         inverse_s, low_s, grad_t, grad_s, student_output, vecs) = forward_both(
            lengths, tokens, jnp.stack([teach_att, stud_att]), jnp.concatenate([teach_ffn, stud_ffn]),
            (teacher_out_bias, teacher_gain, teacher_shift),
            (student_out_bias, student_gain, student_shift),
        )
        def unpack(layer):
            att = gathered[layer]
            qkvt = att[:, :384].reshape(8, 3, 128, -1)
            qkv = [qkvt[:, i].reshape(1024, -1).T for i in range(3)]
            out = att[:, 384:512].reshape(1024, -1)
            f = gathered[2 + 2 * layer : 4 + 2 * layer]
            up = f[:, :, 0:256].transpose(1, 0, 2, 3).reshape(4096, -1).T
            down = f[:, :, 256:512].transpose(1, 0, 2, 3).reshape(4096, -1)
            return (qkv, None, None, out, up, None, down)
        def spread(v):
            return v.reshape(2, 4, rows, 2, 256).transpose(2, 1, 3, 0, 4).reshape(rows, 4096)
        def keep(qkv, slope, hidden, unit, inverse, low, context):
            q, k, v = [qkv[:, :, i * 128:(i + 1) * 128].transpose(1, 0, 2).reshape(pairs, LEN, 16, 64) for i in range(3)]
            scores = jnp.einsum("bqhe,bkhe->bhqk", q, k, preferred_element_type=jnp.float32) * (1.0 / math.sqrt(DH))
            masked = jnp.where(valid[:, None, None, :], scores, masked_fill)
            attention = jax.nn.softmax(masked, axis=-1)
            return [q, k, v, scores, attention, context, unit, inverse, low, hidden, spread(slope), None, None]
        teach, stud = unpack(0), unpack(1)
        ctx = context_s.transpose(1, 0, 2).reshape(rows, -1)
        teach_kept = keep(qkv_t, slope_t, None, unit_t, inverse_t, None, None)
        kept = keep(qkv_s, slope_s, spread(hidden_s), unit_s, inverse_s, low_s, ctx)
    else:
        teach = gather_layer(
            net, teacher_qkv, teacher_qv_bias, teacher_out, teacher_up, teacher_up_bias, teacher_down
        )
        stud = gather_layer(
            net,
            binarize(student_qkv, 0),
            student_qv_bias,
            binarize(student_out, 1),
            binarize(student_up, 0),
            student_up_bias,
            binarize(student_down, 1),
        )
        teach_final, teach_kept = forward(
            tokens, teach, to_float(teacher_out_bias), teach_gain, to_float(teacher_shift), plain_act, valid
        )
        final, kept = forward(tokens, stud, out_bias, gain, shift, clipped_act, valid)
        student_output = to_low(final)
        final_grad = token_valid * (final - teach_final)
        grad_s = norm_back(final_grad, kept[11], kept[12], gain[1])
        grad_t = norm_back(-final_grad, teach_kept[11], teach_kept[12], teach_gain[1])
        vecs = jnp.stack([jnp.sum(grad_s, axis=0), jnp.sum(final_grad * kept[11], axis=0), jnp.sum(final_grad, axis=0)])
    extra = score_weight * jnp.where(pair_valid, kept[3] - teach_kept[3], 0.0)

    second_grad, second_low, pre_grad, pre_low, normed_grad, first_grad = backward_ffn(
        kept, stud, grad_s, gain
    )
    hidden, normed_low, context = kept[9], kept[8], kept[5]
    unit_one = kept[6]
    down_grad = net.sum_dp(net.scatter(cut(to_low(dot_tn(hidden, second_low)), n_mp, 0)))
    up_grad = net.sum_dp(net.scatter(cut(to_low(dot_tn(normed_low, pre_low)), n_mp, 1)))
    first_low = to_low(first_grad)
    out_grad = net.sum_dp(net.scatter(cut(to_low(dot_tn(context, first_low)), n_mp, 0)))
    grads = backward_attention(kept, first_low, stud[3], extra)
    lows = [to_low(item) for item in grads]
    wide = jnp.concatenate(
        [to_low(dot_tn(tokens, item)) for item in lows], axis=0
    )
    qkv_grad = net.sum_dp(net.scatter(cut(wide, n_mp, 1)))
    features = tokens.shape[1]
    qkv_grad = qkv_grad.reshape(3, features, -1).transpose(1, 0, 2)

    teach_second, teach_slow, _, _, _, teach_first = backward_ffn(
        teach_kept, teach, grad_t, teach_gain
    )
    teach_grads = backward_attention(teach_kept, to_low(teach_first), teach[3], -extra)
    teach_lows = [to_low(item) for item in teach_grads]
    input_grad = first_grad + teach_first
    for item, matrix in zip(lows, stud[0]):
        input_grad = input_grad + dot_nt(item, matrix)
    for item, matrix in zip(teach_lows, teach[0]):
        input_grad = input_grad + dot_nt(item, matrix)

    vectors = [
        jnp.sum(first_grad, axis=0),
        vecs[0],
        jnp.sum(normed_grad * unit_one, axis=0),
        vecs[1],
        jnp.sum(normed_grad, axis=0),
        vecs[2],
        net.place(jnp.sum(grads[0], axis=0).reshape(n_mp, -1)).reshape(-1),
        net.place(jnp.sum(grads[2], axis=0).reshape(n_mp, -1)).reshape(-1),
    ]
    wide_vector = net.place(jnp.sum(pre_grad, axis=0).reshape(n_mp, -1)).reshape(-1, features)
    total = net.sum_all(jnp.concatenate([jnp.stack(vectors), wide_vector], axis=0))
    width = features // n_mp
    units = wide_vector.size // n_mp
    return (
        student_output,
        input_grad,
        qkv_grad,
        lax.dynamic_slice_in_dim(total[6:8], me * width, width, axis=1),
        out_grad,
        up_grad,
        lax.dynamic_slice_in_dim(total[8:].reshape(-1), me * units, units),
        down_grad,
        total[0:2],
        total[2:4],
        total[4:6],
    )


def solution(mesh):
    n_dp, n_mp = mesh.shape["dp"], mesh.shape["mp"]

    def body(*args):
        return per_device(n_dp, n_mp, *args)

    return jax.shard_map(
        body,
        mesh=mesh,
        in_specs=(
            P(("dp", "mp"), None),
            P("dp"),
            P(None, None, "mp"),
            P(None, "mp"),
            P("mp", None),
            P(None, "mp"),
            P("mp"),
            P("mp", None),
            P(),
            P(),
            P(),
            P(None, None, "mp"),
            P(None, "mp"),
            P("mp", None),
            P(None, "mp"),
            P("mp"),
            P("mp", None),
            P(),
            P(),
            P(),
        ),
        out_specs=(
            P(("dp", "mp"), None),
            P(("dp", "mp"), None),
            P(None, None, "mp"),
            P(None, "mp"),
            P("mp", None),
            P(None, "mp"),
            P("mp"),
            P("mp", None),
            P(),
            P(),
            P(),
        ),
        check_vma=False,
    )
```

time: 1020 us -> 822 us (0.81)
  waiting for transfers between devices: 591 us -> 154 us
  Pallas kernels: 0 us -> 230 us
  local copies, waits for them, and re-layouts: 87.9 us -> 223 us
  matrix products: 206 us -> 121 us
  blocking collectives: 56 us -> 0 us
  starting transfers between devices: 1.54 us -> 30.9 us
  between operations: 15.5 us -> 2.44 us
    reduce_scatter x7 -> x0, waiting for transfers between devices: 382 us -> none  [the longest x1 65.6 us: per_device(): lax.psum_scatter(stud_back_part.astype(jnp.bfloat16), 'mp', scatter_dimen...]
    pallas_call x0 -> x1, Pallas kernels: none -> 230 us  [forward_both(): pl.pallas_call(forward_kernel, out_shape=[jax.ShapeDtypeStruct(shape, kin...]
    all_gather x7 -> x0, waiting for transfers between devices: 203 us -> none  [the longest x1 45 us: per_device(): lax.all_gather(teach_normed_low, 'mp', axis=0, tiled=True)]
    ppermute x0 -> x49, waiting for transfers between devices: none -> 154 us  [the longest x14 79 us: flip_dp(): return lax.ppermute(values, self.axes, pairs)]
    dot_general x31 -> x28, matrix products: 206 us -> 121 us  [the longest x12 47.7 us: dot_nt(): lax.dot_general(left, right, (((1,), (1,)), ((), ())), preferred_element_...]
    transpose x0 -> x17, local copies, waits for them, and re-layouts: none -> 73.3 us  [the longest x3 39.1 us: unpack(): down = f[:, :, 256:512].transpose(1, 0, 2, 3).reshape(4096, -1)]
    psum x2 -> x0, blocking collectives: 56 us -> none  [the longest x1 42.8 us: per_device(): lax.psum((out_bias_local, gain_local, shift_local), ('dp', 'mp'))]
    convert_element_type x6 -> x15, local copies, waits for them, and re-layouts: 10 us -> 50.3 us  [the longest x5 43.5 us: backward_ffn(): pre_grad = dot_nt(second_low, down) * slope]
  transfers between devices with their start and end apart: 15 -> 49, of which waited for: 14 -> 19; matrix products, arithmetic and copies ran while one was open for 26% -> 43% of each run, Pallas kernels for 0% -> 0%
where the time goes in v1:
time: 822 us; the launch traced here: 815 us
  Pallas kernels  230 us (28%)
  local copies, waits for them, and re-layouts  223 us (27%)
  waiting for transfers between devices  154 us (19%)
  matrix products  121 us (15%)
  other arithmetic  53.9 us (7%)
  starting transfers between devices  30.9 us (4%)
    pallas_call x1, Pallas kernels, forward_both(): pl.pallas_call(forward_kernel, out_shape=[jax.ShapeDtypeStruct(shape, kin...  230 us
    ppermute x14, waiting for transfers between devices, flip_dp(): return lax.ppermute(values, self.axes, pairs)  79 us
    ppermute x35, waiting for transfers between devices, flip(): return lax.ppermute(values, self.axes, pairs)  74.9 us
    dot_general x12, matrix products, dot_nt(): lax.dot_general(left, right, (((1,), (1,)), ((), ())), preferred_element_...  47.7 us
    convert_element_type x5, local copies, waits for them, and re-layouts, backward_ffn(): pre_grad = dot_nt(second_low, down) * slope  43.5 us
    transpose x3, local copies, waits for them, and re-layouts, unpack(): down = f[:, :, 256:512].transpose(1, 0, 2, 3).reshape(4096, -1)  39.1 us
    dot_general x6, matrix products, dot_tn(): lax.dot_general(left, right, (((0,), (0,)), ((), ())), preferred_element_...  21.2 us
    ppermute x35, starting transfers between devices, flip(): return lax.ppermute(values, self.axes, pairs)  20.3 us
  transfers between devices with their start and end apart: 49, of which 19 were waited for; matrix products, arithmetic and copies ran while one was open for 43% of the time, Pallas kernels for 0%

profile of v1, /device:TPU:0, one launch (start us, length us, event | category | flops | bytes accessed | tf_op | source)
XLA Modules:
  0.0 814.7 jit_solution(4981875267631239467)
XLA Ops:
  0.7 3.0 copy.51
  19.2 2.5 pad_maximum_fusion.1.packs_ffn
  21.7 229.9 %forward_both.1 = (bf16[6,8,528,1024]{3,2,1,0:T(8,128)(2,1)}, bf16[8,384,384]{2,1,0:T(8,128)(2,1)}, bf16[8,384,384]{2,1,0:T(8,128)(2,1)}, bf16[4,384,256]{2,1,0:...) custom-call(s32[24]{0:T(128)} %lengths.1, ...), custom_call_target="tpu_custom_call" | custom-call | tf_op jit(solution)/shard_map/forward_both/pallas_call | solution.py:572
  251.6 3.8 reshape.223
  255.4 5.9 copy.93
  261.3 6.9 convolution_convert_fusion
  272.7 22.9 %slice_bitcast_fusion.5 = (bf16[8,2,256,1024]{3,2,0,1:T(8,128)(2,1)}, bf16[8,2,256,1024]{3,2,0,1:T(8,128)(2,1)}, bf16[8,2,256,1024]{3,2,0,1:T(8,128)(2,1)}, bf16[8,2,256,1024]{3,2,0,1:T(8,128)(2,1)}) fusion(bf16[6,8,528,1024]{3,2,1,0:T(8,128)(2,1)} %get-tuple-element.30), kind=kLoop, calls=%fused_computation.9 | loop fusion | bytes 67108864 | tf_op jit(solution)/shard_map/transpose | solution.py:683
  295.6 8.1 copy.52
  303.7 5.9 reshape.230
  309.6 10.3 %copy.53 = f32[384,4,2,2,256]{4,3,2,1,0:T(2,128)} copy(f32[384,4,2,2,256]{4,2,0,1,3:T(2,128)} %bitcast.223) | data formatting | bytes 12582912 | tf_op jit(solution)/shard_map/convert_element_type | solution.py:228
  320.0 9.0 %reshape.225 = f32[384,4096]{1,0:T(8,128)} reshape(f32[384,4,2,2,256]{4,3,2,1,0:T(2,128)} %copy.53) | data formatting | bytes 12582912 | tf_op jit(solution)/shard_map/convert_element_type | solution.py:228
  329.0 8.1 copy.54
  337.1 11.6 %fusion.156 = (f32[4096]{0:T(1024)S(1)}, bf16[384,4096]{1,0:T(8,128)(2,1)}) fusion(f32[384,4096]{1,0:T(8,128)} %reshape.225, bf16[4096,1024]{1,0:T(8,128)(2,1)} %bitcast.227, f32[384,1024]{1,0:T(8,128)S(1)} %copy-done.64), kind=kOutput, calls=%fused_computation.279 | convolution fusion | flops 3226333184 | bytes 19415040 | tf_op jit(solution)/shard_map/dot_general | solution.py:52
  348.7 6.8 multiply_reduce_fusion.2
  362.9 11.9 %slice_bitcast_fusion.1 = (bf16[8,528,1024]{2,1,0:T(8,128)(2,1)}, bf16[8,528,1024]{2,1,0:T(8,128)(2,1)}) fusion(bf16[6,8,528,1024]{3,2,1,0:T(8,128)(2,1)} %get-tuple-element.30), kind=kLoop, calls=%fused_computation.5 | loop fusion | bytes 34603008 | tf_op jit(solution)/shard_map/squeeze | solution.py:677
  383.1 2.7 slice_bitcast_fusion.9
  388.1 3.2 reshape.209
  402.4 3.5 reshape.213
  405.8 3.7 fusion.97
  413.6 3.3 reshape.214
  418.0 3.2 reshape.215
  421.3 6.2 select_multiply_fusion
  427.5 8.4 %bitcast_convert_fusion.1 = (bf16[3,128,16,64]{1,3,2,0:T(8,128)(2,1)}, f32[3,16,64,128]{3,2,1,0:T(8,128)}) fusion(f32[3,16,128,128]{2,3,1,0:T(8,128)} %get-tuple-element.128, f32[3,16,128,128]{2,3,1,0:T(8,128)} %fusion.97, f32[3,16,128,128]{2,3,1,0:T(8,128)} %copy-done.66, f32[3,16,128]{2,1,0:T(8,128)S(1)} %get-tuple-element.134, ...), kind=kOutput, calls=%fused_computation.58 | convolution fusion | flops 106961024 | bytes 12607488 | tf_op jit(solution)/shard_map/bhqk,bkhe->bqhe/dot_general | solution.py:248
  438.7 7.7 fusion.58
  446.4 6.1 slice.277
  452.5 3.1 slice.281
  455.6 6.1 slice.282
  461.7 8.1 copy.55
  469.8 7.5 reshape.231
  477.3 10.8 %copy.56 = f32[2,4,384,2,256]{2,4,0,3,1:T(8,128)} copy(f32[2,4,384,2,256]{4,3,2,1,0:T(2,128)} %reshape.231) | data formatting | bytes 12582912 | tf_op jit(solution)/shard_map/convert_element_type | solution.py:228
  488.1 8.2 %copy.57 = bf16[8,2,256,1024]{3,2,1,0:T(8,128)(2,1)} copy(bf16[8,2,256,1024]{3,2,0,1:T(8,128)(2,1)} %get-tuple-element.52) | data formatting | bytes 16777216 | tf_op jit(solution)/shard_map/transpose | solution.py:682
  496.3 9.9 %fusion.4 = bf16[384,4096]{0,1:T(8,128)(2,1)S(1)} fusion(f32[2,4,384,2,256]{2,4,0,3,1:T(8,128)} %copy.56, bf16[4096,1024]{1,0:T(8,128)(2,1)} %bitcast.228, f32[384,1024]{1,0:T(8,128)S(1)} %copy-done.35), kind=kOutput, calls=%fused_computation.14 | convolution fusion | flops 3224764416 | bytes 19398656 | tf_op jit(solution)/shard_map/dot_general | solution.py:52
  506.2 4.7 fusion.135
  511.0 4.0 convolution_convert_fusion.3
  515.1 3.2 reshape.233
  518.3 2.6 copy.81
  520.9 5.7 fusion.152
  528.9 3.4 reshape.219
  532.3 3.9 fusion.95
  538.3 8.0 fusion.61
  546.4 8.0 fusion.64
  556.3 4.2 convert_bitcast_fusion.2
  561.2 2.6 convert_bitcast_fusion.1
  581.8 12.0 %pad_maximum_fusion = bf16[3072,1024]{1,0:T(8,128)(2,1)S(1)} fusion(bf16[1024,1024]{1,0:T(8,128)(2,1)S(1)} %convert_bitcast_fusion, bf16[1024,1024]{1,0:T(8,128)(2,1)S(1)} %copy-done.27, bf16[1024,1024]{1,0:T(8,128)(2,1)S(1)} %copy-done.26), kind=kLoop, calls=%fused_computation.12 | loop fusion | flops 18874368 | bytes 12582912 | tf_op jit(solution)/shard_map/concatenate | solution.py:732
  603.4 5.0 convolution_convert_fusion.1
  608.4 2.6 collective-permute-start.15
  613.3 4.2 collective-permute-done.22
  622.3 2.6 collective-permute-done.23
  628.0 3.3 collective-permute-done.24
  634.9 6.6 collective-permute-done.25
  642.8 3.9 convert_add_fusion.2
  650.4 3.3 collective-permute-done.26
  654.4 4.4 collective-permute-done.3
  661.1 8.8 %collective-permute-done.41 = bf16[256,1024]{1,0:T(8,128)(2,1)S(1)} collective-permute-done((bf16[256,1024]{1,0:T(8,128)(2,1)S(1)}, bf16[256,1024]{1,0:T(8,128)(2,1)S(1)}, u32[]{:S(2)}, u32[]{:S(2)}) %collective-permute-start.41) | collective-permute-done | bytes 524320 | tf_op jit(solution)/shard_map/ppermute | solution.py:68
  672.6 8.6 %collective-permute-done.30 = bf16[512,512]{1,0:T(8,128)(2,1)S(1)} collective-permute-done((bf16[512,512]{1,0:T(8,128)(2,1)S(1)}, bf16[512,512]{1,0:T(8,128)(2,1)S(1)}, u32[]{:S(2)}, u32[]{:S(2)}) %collective-permute-start.30) | collective-permute-done | bytes 524320 | tf_op jit(solution)/shard_map/ppermute | solution.py:68
  682.1 8.4 %collective-permute-done.4 = bf16[3072,128]{1,0:T(8,128)(2,1)S(1)} collective-permute-done((bf16[3072,128]{1,0:T(8,128)(2,1)S(1)}, bf16[3072,128]{1,0:T(8,128)(2,1)S(1)}, u32[]{:S(2)}, u32[]{:S(2)}) %collective-permute-start.4) | collective-permute-done | bytes 786464 | tf_op jit(solution)/shard_map/ppermute | solution.py:68
  690.9 6.1 collective-permute-done.7
  702.5 6.9 collective-permute-done.8
  711.5 12.6 %collective-permute-done.42 = bf16[512,1024]{1,0:T(8,128)(2,1)S(1)} collective-permute-done((bf16[512,1024]{1,0:T(8,128)(2,1)S(1)}, bf16[512,1024]{1,0:T(8,128)(2,1)S(1)}, u32[]{:S(2)}, u32[]{:S(2)}) %collective-permute-start.42) | collective-permute-done | bytes 1048608 | tf_op jit(solution)/shard_map/ppermute | solution.py:68
  727.3 16.5 %collective-permute-done.31 = bf16[1024,512]{1,0:T(8,128)(2,1)S(1)} collective-permute-done((bf16[1024,512]{1,0:T(8,128)(2,1)S(1)}, bf16[1024,512]{1,0:T(8,128)(2,1)S(1)}, u32[]{:S(2)}, u32[]{:S(2)}) %collective-permute-start.31) | collective-permute-done | bytes 1048608 | tf_op jit(solution)/shard_map/ppermute | solution.py:68
  747.0 23.7 %collective-permute-done.35 = bf16[512,512]{1,0:T(8,128)(2,1)S(1)} collective-permute-done((bf16[512,512]{1,0:T(8,128)(2,1)S(1)}, bf16[512,512]{1,0:T(8,128)(2,1)S(1)}, u32[]{:S(2)}, u32[]{:S(2)}) %collective-permute-start.35) | collective-permute-done | bytes 524320 | tf_op jit(solution)/shard_map/ppermute | solution.py:74
  771.0 5.4 collective-permute-done.10
  779.1 18.8 %collective-permute-done.36 = bf16[512,512]{1,0:T(8,128)(2,1)S(1)} collective-permute-done((bf16[512,512]{1,0:T(8,128)(2,1)S(1)}, bf16[512,512]{1,0:T(8,128)(2,1)S(1)}, u32[]{:S(2)}, u32[]{:S(2)}) %collective-permute-start.36) | collective-permute-done | bytes 524320 | tf_op jit(solution)/shard_map/ppermute | solution.py:74
  801.1 10.8 %collective-permute-done.37 = bf16[512,512]{1,0:T(8,128)(2,1)S(1)} collective-permute-done((bf16[512,512]{1,0:T(8,128)(2,1)S(1)}, bf16[512,512]{1,0:T(8,128)(2,1)S(1)}, u32[]{:S(2)}, u32[]{:S(2)}) %collective-permute-start.37) | collective-permute-done | bytes 524320 | tf_op jit(solution)/shard_map/ppermute | solution.py:74
  (398 shorter events, 139.0 us)
Async XLA Ops:
  272.7 368.9 %collective-permute-start.39 = (bf16[512,1024]{1,0:T(8,128)(2,1)}, bf16[512,1024]{1,0:T(8,128)(2,1)}, u32[]{:S(2)}, u32[]{:S(2)}) collective-permute-start(bf16[512,1024]{1,0:T(8,128)(2,1)} %get-tuple-element.60), channel_id=1, source_target_pairs={{0,1},{1,0},{2,3},{3,2},{4,5},{5,4},{6,7},{7,6},{8,9},{9,8},{10,11... | collective-permute-start | bytes 3145736 | tf_op jit(solution)/shard_map/ppermute | solution.py:68
  295.6 8.1 copy-start.23
  337.1 11.6 %copy-start.5 = (bf16[8,2,256,1024]{3,2,1,0:T(8,128)(2,1)S(1)}, bf16[8,2,256,1024]{3,2,1,0:T(8,128)(2,1)}, u32[]{:S(2)}) copy-start(bf16[8,2,256,1024]{3,2,1,0:T(8,128)(2,1)} %copy.54) | copy-start | bytes 25165828
  337.1 11.6 %copy-start.36 = (f32[384,1024]{1,0:T(8,128)S(1)}, f32[384,1024]{1,0:T(8,128)}, u32[]{:S(2)}) copy-start(f32[384,1024]{1,0:T(8,128)} %get-tuple-element.32) | copy-start | bytes 4718596
  361.9 236.8 %collective-permute-start.17 = (bf16[128,1024]{1,0:T(8,128)(2,1)}, bf16[128,1024]{1,0:T(8,128)(2,1)}, u32[]{:S(2)}, u32[]{:S(2)}) collective-permute-start(bf16[128,1024]{1,0:T(8,128)(2,1)} %get-tuple-element.93), channel_id=1, source_target_pairs={{0,1},{1,0},{2,3},{3,2},{4,5},{5,4},{6,7},{7,6},{8,9},{9,8},{10,11... | collective-permute-start | bytes 786440 | tf_op jit(solution)/shard_map/ppermute | solution.py:68
  362.4 238.0 %collective-permute-start.18 = (bf16[128,1024]{1,0:T(8,128)(2,1)}, bf16[128,1024]{1,0:T(8,128)(2,1)}, u32[]{:S(2)}, u32[]{:S(2)}) collective-permute-start(bf16[128,1024]{1,0:T(8,128)(2,1)} %get-tuple-element.92), channel_id=1, source_target_pairs={{0,1},{1,0},{2,3},{3,2},{4,5},{5,4},{6,7},{7,6},{8,9},{9,8},{10,11... | collective-permute-start | bytes 786440 | tf_op jit(solution)/shard_map/ppermute | solution.py:68
  362.4 237.9 %collective-permute-start.21 = (bf16[128,1024]{1,0:T(8,128)(2,1)}, bf16[128,1024]{1,0:T(8,128)(2,1)}, u32[]{:S(2)}, u32[]{:S(2)}) collective-permute-start(bf16[128,1024]{1,0:T(8,128)(2,1)} %get-tuple-element.91), channel_id=1, source_target_pairs={{0,1},{1,0},{2,3},{3,2},{4,5},{5,4},{6,7},{7,6},{8,9},{9,8},{10,11... | collective-permute-start | bytes 786440 | tf_op jit(solution)/shard_map/ppermute | solution.py:68
  438.6 142.5 %collective-permute-start.11 = (f32[12,1024]{1,0:T(8,128)S(1)}, f32[12,1024]{1,0:T(8,128)S(1)}, u32[]{:S(2)}, u32[]{:S(2)}) collective-permute-start(f32[12,1024]{1,0:T(8,128)S(1)} %concatenate.90), channel_id=1, source_target_pairs={{0,1},{1,0},{2,3},{3,2},{4,5},{5,4},{6,7},{7,6},{8,9},{9,8},{10,11... | collective-permute-start | bytes 147464 | tf_op jit(solution)/shard_map/ppermute | solution.py:68
  488.1 8.2 %copy-start.35 = (f32[384,1024]{1,0:T(8,128)S(1)}, f32[384,1024]{1,0:T(8,128)}, u32[]{:S(2)}) copy-start(f32[384,1024]{1,0:T(8,128)} %get-tuple-element.34) | copy-start | bytes 4718596
  496.2 9.9 %copy-start = (bf16[8,2,256,1024]{3,2,1,0:T(8,128)(2,1)S(1)}, bf16[8,2,256,1024]{3,2,1,0:T(8,128)(2,1)}, u32[]{:S(2)}) copy-start(bf16[8,2,256,1024]{3,2,1,0:T(8,128)(2,1)} %copy.57) | copy-start | bytes 25165828
  496.2 9.9 %copy-start.11 = (f32[384,1024]{1,0:T(8,128)S(1)}, f32[384,1024]{1,0:T(8,128)}, u32[]{:S(2)}) copy-start(f32[384,1024]{1,0:T(8,128)} %get-tuple-element.36) | copy-start | bytes 4718596
  556.3 9.0 %slice-start.2 = ((s8[6291456]{0:T(1024)(128)(4,1)}), s8[4194304]{0:T(1024)(128)(4,1)S(1)}, s32[]{:S(2)}) async-start(s8[6291456]{0:T(1024)(128)(4,1)} %bitcast.220), calls=%async_computation.2 | async-start | bytes 8388608
  564.5 9.2 %copy-start.14 = (bf16[3,128,16,64]{1,0,3,2:T(4,128)(2,1)}, bf16[3,128,16,64]{1,0,3,2:T(4,128)(2,1)S(1)}, u32[]{:S(2)}) copy-start(bf16[3,128,16,64]{1,0,3,2:T(4,128)(2,1)S(1)} %copy.78) | copy-start | bytes 2359300
  581.2 12.7 %collective-permute-start.12 = (f32[12,1024]{1,0:T(8,128)S(1)}, f32[12,1024]{1,0:T(8,128)S(1)}, u32[]{:S(2)}, u32[]{:S(2)}) collective-permute-start(f32[12,1024]{1,0:T(8,128)S(1)} %add.255), channel_id=1, source_target_pairs={{0,2},{1,3},{2,0},{3,1},{4,6},{5,7},{6,4},{7,5},{8,10},{9,11},{10,... | collective-permute-start | bytes 147464 | tf_op jit(solution)/shard_map/ppermute | solution.py:68
  593.9 4.7 collective-permute-start.13
  598.5 23.3 %collective-permute-start.16 = (bf16[128,1024]{1,0:T(8,128)(2,1)}, bf16[128,1024]{1,0:T(8,128)(2,1)}, u32[]{:S(2)}, u32[]{:S(2)}) collective-permute-start(bf16[128,1024]{1,0:T(8,128)(2,1)} %get-tuple-element.90), channel_id=1, source_target_pairs={{0,1},{1,0},{2,3},{3,2},{4,5},{5,4},{6,7},{7,6},{8,9},{9,8},{10,11... | collective-permute-start | bytes 786440 | tf_op jit(solution)/shard_map/ppermute | solution.py:68
  598.7 9.6 %collective-permute-start.14 = (f32[12,1024]{1,0:T(8,128)S(1)}, f32[12,1024]{1,0:T(8,128)S(1)}, u32[]{:S(2)}, u32[]{:S(2)}) collective-permute-start(f32[12,1024]{1,0:T(8,128)S(1)} %add.257), channel_id=1, source_target_pairs={{0,8},{1,9},{2,10},{3,11},{4,12},{5,13},{6,14},{7,15},{8,0},{9,1},... | collective-permute-start | bytes 147464 | tf_op jit(solution)/shard_map/ppermute | solution.py:74
  601.8 9.8 %collective-permute-start.19 = (bf16[64,1024]{1,0:T(8,128)(2,1)S(1)}, bf16[64,1024]{1,0:T(8,128)(2,1)S(1)}, u32[]{:S(2)}, u32[]{:S(2)}) collective-permute-start(bf16[64,1024]{1,0:T(8,128)(2,1)S(1)} %get-tuple-element.119), channel_id=1, source_target_pairs={{0,4},{1,5},{2,6},{3,7},{4,0},{5,1},{6,2},{7,3},{8,12},{9,13},{10,... | collective-permute-start | bytes 393224 | tf_op jit(solution)/shard_map/ppermute | solution.py:68
  608.3 10.5 %copy-start.4 = (bf16[1024,4096]{1,0:T(8,128)(2,1)}, bf16[1024,4096]{1,0:T(8,128)(2,1)S(1)}, u32[]{:S(2)}) copy-start(bf16[1024,4096]{1,0:T(8,128)(2,1)S(1)} %convolution_convert_fusion.1) | copy-start | bytes 25165828
  608.4 12.7 %collective-permute-start.15 = (f32[12,1024]{1,0:T(8,128)S(1)}, f32[12,1024]{1,0:T(8,128)S(1)}, u32[]{:S(2)}, u32[]{:S(2)}) collective-permute-start(f32[12,1024]{1,0:T(8,128)S(1)} %add.258), channel_id=1, source_target_pairs={{0,16},{1,17},{2,18},{3,19},{4,20},{5,21},{6,22},{7,23},{8,24},{9,... | collective-permute-start | bytes 147464 | tf_op jit(solution)/shard_map/ppermute | solution.py:74
  611.0 6.5 collective-permute-start.22
  611.7 10.6 %collective-permute-start.20 = (bf16[128,1024]{1,0:T(8,128)(2,1)S(1)}, bf16[128,1024]{1,0:T(8,128)(2,1)}, u32[]{:S(2)}, u32[]{:S(2)}) collective-permute-start(bf16[128,1024]{1,0:T(8,128)(2,1)S(1)} %pad_maximum_fusion.10), channel_id=1, source_target_pairs={{0,2},{1,3},{2,0},{3,1},{4,6},{5,7},{6,4},{7,5},{8,10},{9,11},{10,... | collective-permute-start | bytes 786440 | tf_op jit(solution)/shard_map/ppermute | solution.py:68
  618.3 6.7 collective-permute-start.23
  621.1 10.3 %copy-start.39 = (bf16[512,1024]{1,0:T(8,128)(2,1)S(1)}, bf16[512,1024]{1,0:T(8,128)(2,1)}, u32[]{:S(2)}) copy-start(bf16[512,1024]{1,0:T(8,128)(2,1)} %get-tuple-element.58) | copy-start | bytes 3145732
  621.1 10.3 %copy-start.40 = (bf16[512,1024]{1,0:T(8,128)(2,1)S(1)}, bf16[512,1024]{1,0:T(8,128)(2,1)}, u32[]{:S(2)}) copy-start(bf16[512,1024]{1,0:T(8,128)(2,1)} %get-tuple-element.59) | copy-start | bytes 3145732
  621.1 10.3 %collective-permute-start.1 = (bf16[3072,128]{1,0:T(8,128)(2,1)}, bf16[3072,128]{1,0:T(8,128)(2,1)S(1)}, u32[]{:S(2)}, u32[]{:S(2)}) collective-permute-start(bf16[3072,128]{1,0:T(8,128)(2,1)} %get-tuple-element.74), channel_id=1, source_target_pairs={{0,1},{1,0},{2,3},{3,2},{4,5},{5,4},{6,7},{7,6},{8,9},{9,8},{10,11... | collective-permute-start | bytes 2359304 | tf_op jit(solution)/shard_map/ppermute | solution.py:68
  621.8 10.2 %collective-permute-start.2 = (bf16[3072,128]{1,0:T(8,128)(2,1)}, bf16[3072,128]{1,0:T(8,128)(2,1)S(1)}, u32[]{:S(2)}, u32[]{:S(2)}) collective-permute-start(bf16[3072,128]{1,0:T(8,128)(2,1)} %get-tuple-element.73), channel_id=1, source_target_pairs={{0,1},{1,0},{2,3},{3,2},{4,5},{5,4},{6,7},{7,6},{8,9},{9,8},{10,11... | collective-permute-start | bytes 2359304 | tf_op jit(solution)/shard_map/ppermute | solution.py:68
  622.3 9.8 %collective-permute-start.5 = (bf16[3072,128]{1,0:T(8,128)(2,1)}, bf16[3072,128]{1,0:T(8,128)(2,1)S(1)}, u32[]{:S(2)}, u32[]{:S(2)}) collective-permute-start(bf16[3072,128]{1,0:T(8,128)(2,1)} %get-tuple-element.72), channel_id=1, source_target_pairs={{0,1},{1,0},{2,3},{3,2},{4,5},{5,4},{6,7},{7,6},{8,9},{9,8},{10,11... | collective-permute-start | bytes 2359304 | tf_op jit(solution)/shard_map/ppermute | solution.py:68
  626.3 5.0 collective-permute-start.24
  631.3 10.8 %collective-permute-start.40 = (bf16[512,1024]{1,0:T(8,128)(2,1)S(1)}, bf16[512,1024]{1,0:T(8,128)(2,1)S(1)}, u32[]{:S(2)}, u32[]{:S(2)}) collective-permute-start(bf16[512,1024]{1,0:T(8,128)(2,1)S(1)} %copy-done.40), channel_id=1, source_target_pairs={{0,1},{1,0},{2,3},{3,2},{4,5},{5,4},{6,7},{7,6},{8,9},{9,8},{10,11... | collective-permute-start | bytes 3145736 | tf_op jit(solution)/shard_map/ppermute | solution.py:68
  631.4 10.9 %collective-permute-start.43 = (bf16[512,1024]{1,0:T(8,128)(2,1)S(1)}, bf16[512,1024]{1,0:T(8,128)(2,1)S(1)}, u32[]{:S(2)}, u32[]{:S(2)}) collective-permute-start(bf16[512,1024]{1,0:T(8,128)(2,1)S(1)} %copy-done.39), channel_id=1, source_target_pairs={{0,1},{1,0},{2,3},{3,2},{4,5},{5,4},{6,7},{7,6},{8,9},{9,8},{10,11... | collective-permute-start | bytes 3145736 | tf_op jit(solution)/shard_map/ppermute | solution.py:68
  632.0 9.5 %copy-start.43 = (bf16[1024,512]{1,0:T(8,128)(2,1)S(1)}, bf16[1024,512]{1,0:T(8,128)(2,1)}, u32[]{:S(2)}) copy-start(bf16[1024,512]{1,0:T(8,128)(2,1)} %get-tuple-element.66) | copy-start | bytes 3145732
  632.0 9.6 %copy-start.42 = (bf16[1024,512]{1,0:T(8,128)(2,1)S(1)}, bf16[1024,512]{1,0:T(8,128)(2,1)}, u32[]{:S(2)}) copy-start(bf16[1024,512]{1,0:T(8,128)(2,1)} %get-tuple-element.65) | copy-start | bytes 3145732
  632.0 14.7 %collective-permute-start.28 = (bf16[1024,512]{1,0:T(8,128)(2,1)}, bf16[1024,512]{1,0:T(8,128)(2,1)S(1)}, u32[]{:S(2)}, u32[]{:S(2)}) collective-permute-start(bf16[1024,512]{1,0:T(8,128)(2,1)} %get-tuple-element.67), channel_id=1, source_target_pairs={{0,1},{1,0},{2,3},{3,2},{4,5},{5,4},{6,7},{7,6},{8,9},{9,8},{10,11... | collective-permute-start | bytes 3145736 | tf_op jit(solution)/shard_map/ppermute | solution.py:68
  632.1 9.4 %collective-permute-start.25 = (bf16[64,1024]{1,0:T(8,128)(2,1)S(1)}, bf16[64,1024]{1,0:T(8,128)(2,1)S(1)}, u32[]{:S(2)}, u32[]{:S(2)}) collective-permute-start(bf16[64,1024]{1,0:T(8,128)(2,1)S(1)} %fusion.126), channel_id=1, source_target_pairs={{0,16},{1,17},{2,18},{3,19},{4,20},{5,21},{6,22},{7,23},{8,24},{9,... | collective-permute-start | bytes 393224 | tf_op jit(solution)/shard_map/ppermute | solution.py:74
  634.8 14.0 %slice-start.4 = ((s8[8388608]{0:T(1024)(128)(4,1)}), s8[4194304]{0:T(1024)(128)(4,1)S(1)}, s32[]{:S(2)}) async-start(s8[8388608]{0:T(1024)(128)(4,1)} %bitcast.224), calls=%async_computation.4 | async-start | bytes 8388608
  641.5 5.8 collective-permute-start.29
  641.6 7.2 collective-permute-start.32
  642.2 59.8 %collective-permute-start.38 = (bf16[512,1024]{1,0:T(8,128)(2,1)S(1)}, bf16[512,1024]{1,0:T(8,128)(2,1)S(1)}, u32[]{:S(2)}, u32[]{:S(2)}) collective-permute-start(bf16[512,1024]{1,0:T(8,128)(2,1)S(1)} %copy-done.38), channel_id=1, source_target_pairs={{0,1},{1,0},{2,3},{3,2},{4,5},{5,4},{6,7},{7,6},{8,9},{9,8},{10,11... | collective-permute-start | bytes 3145736 | tf_op jit(solution)/shard_map/ppermute | solution.py:68
  642.3 39.2 %collective-permute-start = (bf16[3072,128]{1,0:T(8,128)(2,1)S(1)}, bf16[3072,128]{1,0:T(8,128)(2,1)S(1)}, u32[]{:S(2)}, u32[]{:S(2)}) collective-permute-start(bf16[3072,128]{1,0:T(8,128)(2,1)S(1)} %copy-done.44), channel_id=1, source_target_pairs={{0,1},{1,0},{2,3},{3,2},{4,5},{5,4},{6,7},{7,6},{8,9},{9,8},{10,11... | collective-permute-start | bytes 2359304 | tf_op jit(solution)/shard_map/ppermute | solution.py:68
  646.7 12.0 %collective-permute-start.3 = (bf16[1536,128]{1,0:T(8,128)(2,1)S(1)}, bf16[1536,128]{1,0:T(8,128)(2,1)S(1)}, u32[]{:S(2)}, u32[]{:S(2)}) collective-permute-start(bf16[1536,128]{1,0:T(8,128)(2,1)S(1)} %get-tuple-element.115), channel_id=1, source_target_pairs={{0,4},{1,5},{2,6},{3,7},{4,0},{5,1},{6,2},{7,3},{8,12},{9,13},{10,... | collective-permute-start | bytes 1179656 | tf_op jit(solution)/shard_map/ppermute | solution.py:68
  647.3 12.0 %collective-permute-start.6 = (bf16[1536,128]{1,0:T(8,128)(2,1)S(1)}, bf16[1536,128]{1,0:T(8,128)(2,1)S(1)}, u32[]{:S(2)}, u32[]{:S(2)}) collective-permute-start(bf16[1536,128]{1,0:T(8,128)(2,1)S(1)} %get-tuple-element.116), channel_id=1, source_target_pairs={{0,2},{1,3},{2,0},{3,1},{4,6},{5,7},{6,4},{7,5},{8,10},{9,11},{10,... | collective-permute-start | bytes 1179656 | tf_op jit(solution)/shard_map/ppermute | solution.py:68
  648.8 5.0 collective-permute-start.26
  653.8 16.2 %collective-permute-start.41 = (bf16[256,1024]{1,0:T(8,128)(2,1)S(1)}, bf16[256,1024]{1,0:T(8,128)(2,1)S(1)}, u32[]{:S(2)}, u32[]{:S(2)}) collective-permute-start(bf16[256,1024]{1,0:T(8,128)(2,1)S(1)} %get-tuple-element.99), channel_id=1, source_target_pairs={{0,4},{1,5},{2,6},{3,7},{4,0},{5,1},{6,2},{7,3},{8,12},{9,13},{10,... | collective-permute-start | bytes 1572872 | tf_op jit(solution)/shard_map/ppermute | solution.py:68
  658.7 12.0 %collective-permute-start.44 = (bf16[256,1024]{1,0:T(8,128)(2,1)S(1)}, bf16[256,1024]{1,0:T(8,128)(2,1)S(1)}, u32[]{:S(2)}, u32[]{:S(2)}) collective-permute-start(bf16[256,1024]{1,0:T(8,128)(2,1)S(1)} %get-tuple-element.100), channel_id=1, source_target_pairs={{0,2},{1,3},{2,0},{3,1},{4,6},{5,7},{6,4},{7,5},{8,10},{9,11},{10,... | collective-permute-start | bytes 1572872 | tf_op jit(solution)/shard_map/ppermute | solution.py:68
  659.3 21.9 %collective-permute-start.30 = (bf16[512,512]{1,0:T(8,128)(2,1)S(1)}, bf16[512,512]{1,0:T(8,128)(2,1)S(1)}, u32[]{:S(2)}, u32[]{:S(2)}) collective-permute-start(bf16[512,512]{1,0:T(8,128)(2,1)S(1)} %get-tuple-element.103), channel_id=1, source_target_pairs={{0,4},{1,5},{2,6},{3,7},{4,0},{5,1},{6,2},{7,3},{8,12},{9,13},{10,... | collective-permute-start | bytes 1572872 | tf_op jit(solution)/shard_map/ppermute | solution.py:68
  670.0 20.5 %collective-permute-start.4 = (bf16[3072,128]{1,0:T(8,128)(2,1)S(1)}, bf16[3072,128]{1,0:T(8,128)(2,1)S(1)}, u32[]{:S(2)}, u32[]{:S(2)}) collective-permute-start(bf16[3072,128]{1,0:T(8,128)(2,1)S(1)} %pad_maximum_fusion.7), channel_id=1, source_target_pairs={{0,2},{1,3},{2,0},{3,1},{4,6},{5,7},{6,4},{7,5},{8,10},{9,11},{10,... | collective-permute-start | bytes 2359304 | tf_op jit(solution)/shard_map/ppermute | solution.py:68
  670.7 10.5 %copy-start.41 = (bf16[1024,512]{1,0:T(8,128)(2,1)S(1)}, bf16[1024,512]{1,0:T(8,128)(2,1)}, u32[]{:S(2)}) copy-start(bf16[1024,512]{1,0:T(8,128)(2,1)} %get-tuple-element.64) | copy-start | bytes 3145732
  670.7 26.3 %collective-permute-start.7 = (bf16[3072,128]{1,0:T(8,128)(2,1)S(1)}, bf16[3072,128]{1,0:T(8,128)(2,1)S(1)}, u32[]{:S(2)}, u32[]{:S(2)}) collective-permute-start(bf16[3072,128]{1,0:T(8,128)(2,1)S(1)} %pad_maximum_fusion.8), channel_id=1, source_target_pairs={{0,4},{1,5},{2,6},{3,7},{4,0},{5,1},{6,2},{7,3},{8,12},{9,13},{10,... | collective-permute-start | bytes 2359304 | tf_op jit(solution)/shard_map/ppermute | solution.py:68
  681.2 46.1 %collective-permute-start.27 = (bf16[1024,512]{1,0:T(8,128)(2,1)S(1)}, bf16[1024,512]{1,0:T(8,128)(2,1)S(1)}, u32[]{:S(2)}, u32[]{:S(2)}) collective-permute-start(bf16[1024,512]{1,0:T(8,128)(2,1)S(1)} %copy-done.41), channel_id=1, source_target_pairs={{0,1},{1,0},{2,3},{3,2},{4,5},{5,4},{6,7},{7,6},{8,9},{9,8},{10,11... | collective-permute-start | bytes 3145736 | tf_op jit(solution)/shard_map/ppermute | solution.py:68
  681.5 20.2 %collective-permute-start.33 = (bf16[512,512]{1,0:T(8,128)(2,1)S(1)}, bf16[512,512]{1,0:T(8,128)(2,1)S(1)}, u32[]{:S(2)}, u32[]{:S(2)}) collective-permute-start(bf16[512,512]{1,0:T(8,128)(2,1)S(1)} %get-tuple-element.104), channel_id=1, source_target_pairs={{0,2},{1,3},{2,0},{3,1},{4,6},{5,7},{6,4},{7,5},{8,10},{9,11},{10,... | collective-permute-start | bytes 1572872 | tf_op jit(solution)/shard_map/ppermute | solution.py:68
  690.4 33.7 %collective-permute-start.42 = (bf16[512,1024]{1,0:T(8,128)(2,1)S(1)}, bf16[512,1024]{1,0:T(8,128)(2,1)S(1)}, u32[]{:S(2)}, u32[]{:S(2)}) collective-permute-start(bf16[512,1024]{1,0:T(8,128)(2,1)S(1)} %pad_maximum_fusion.5), channel_id=1, source_target_pairs={{0,2},{1,3},{2,0},{3,1},{4,6},{5,7},{6,4},{7,5},{8,10},{9,11},{10,... | collective-permute-start | bytes 3145736 | tf_op jit(solution)/shard_map/ppermute | solution.py:68
  697.1 27.1 %collective-permute-start.45 = (bf16[512,1024]{1,0:T(8,128)(2,1)S(1)}, bf16[512,1024]{1,0:T(8,128)(2,1)S(1)}, u32[]{:S(2)}, u32[]{:S(2)}) collective-permute-start(bf16[512,1024]{1,0:T(8,128)(2,1)S(1)} %pad_maximum_fusion.6), channel_id=1, source_target_pairs={{0,4},{1,5},{2,6},{3,7},{4,0},{5,1},{6,2},{7,3},{8,12},{9,13},{10,... | collective-permute-start | bytes 3145736 | tf_op jit(solution)/shard_map/ppermute | solution.py:68
  701.7 7.8 collective-permute-start.8
  701.9 41.8 %collective-permute-start.31 = (bf16[1024,512]{1,0:T(8,128)(2,1)S(1)}, bf16[1024,512]{1,0:T(8,128)(2,1)S(1)}, u32[]{:S(2)}, u32[]{:S(2)}) collective-permute-start(bf16[1024,512]{1,0:T(8,128)(2,1)S(1)} %pad_maximum_fusion.3), channel_id=1, source_target_pairs={{0,2},{1,3},{2,0},{3,1},{4,6},{5,7},{6,4},{7,5},{8,10},{9,11},{10,... | collective-permute-start | bytes 3145736 | tf_op jit(solution)/shard_map/ppermute | solution.py:68
  709.5 34.3 %collective-permute-start.34 = (bf16[1024,512]{1,0:T(8,128)(2,1)S(1)}, bf16[1024,512]{1,0:T(8,128)(2,1)S(1)}, u32[]{:S(2)}, u32[]{:S(2)}) collective-permute-start(bf16[1024,512]{1,0:T(8,128)(2,1)S(1)} %pad_maximum_fusion.4), channel_id=1, source_target_pairs={{0,4},{1,5},{2,6},{3,7},{4,0},{5,1},{6,2},{7,3},{8,12},{9,13},{10,... | collective-permute-start | bytes 3145736 | tf_op jit(solution)/shard_map/ppermute | solution.py:68
  724.2 20.4 %collective-permute-start.9 = (bf16[1536,128]{1,0:T(8,128)(2,1)S(1)}, bf16[1536,128]{1,0:T(8,128)(2,1)S(1)}, u32[]{:S(2)}, u32[]{:S(2)}) collective-permute-start(bf16[1536,128]{1,0:T(8,128)(2,1)S(1)} %fusion.119), channel_id=1, source_target_pairs={{0,16},{1,17},{2,18},{3,19},{4,20},{5,21},{6,22},{7,23},{8,24},{9,... | collective-permute-start | bytes 1179656 | tf_op jit(solution)/shard_map/ppermute | solution.py:74
  726.3 20.5 %collective-permute-start.46 = (bf16[256,1024]{1,0:T(8,128)(2,1)S(1)}, bf16[256,1024]{1,0:T(8,128)(2,1)S(1)}, u32[]{:S(2)}, u32[]{:S(2)}) collective-permute-start(bf16[256,1024]{1,0:T(8,128)(2,1)S(1)} %dynamic-slice_convert_fusion), channel_id=1, source_target_pairs={{0,8},{1,9},{2,10},{3,11},{4,12},{5,13},{6,14},{7,15},{8,0},{9,1},... | collective-permute-start | bytes 1572872 | tf_op jit(solution)/shard_map/ppermute | solution.py:74
  744.5 26.3 %collective-permute-start.35 = (bf16[512,512]{1,0:T(8,128)(2,1)S(1)}, bf16[512,512]{1,0:T(8,128)(2,1)S(1)}, u32[]{:S(2)}, u32[]{:S(2)}) collective-permute-start(bf16[512,512]{1,0:T(8,128)(2,1)S(1)} %dynamic-slice_convert_fusion.1), channel_id=1, source_target_pairs={{0,8},{1,9},{2,10},{3,11},{4,12},{5,13},{6,14},{7,15},{8,0},{9,1},... | collective-permute-start | bytes 1572872 | tf_op jit(solution)/shard_map/ppermute | solution.py:74
  744.7 31.6 %collective-permute-start.10 = (bf16[1536,128]{1,0:T(8,128)(2,1)S(1)}, bf16[1536,128]{1,0:T(8,128)(2,1)S(1)}, u32[]{:S(2)}, u32[]{:S(2)}) collective-permute-start(bf16[1536,128]{1,0:T(8,128)(2,1)S(1)} %add_convert_fusion.7), channel_id=1, source_target_pairs={{0,8},{1,9},{2,10},{3,11},{4,12},{5,13},{6,14},{7,15},{8,0},{9,1},... | collective-permute-start | bytes 1179656 | tf_op jit(solution)/shard_map/ppermute | solution.py:74
  746.9 29.7 %collective-permute-start.47 = (bf16[256,1024]{1,0:T(8,128)(2,1)S(1)}, bf16[256,1024]{1,0:T(8,128)(2,1)S(1)}, u32[]{:S(2)}, u32[]{:S(2)}) collective-permute-start(bf16[256,1024]{1,0:T(8,128)(2,1)S(1)} %fusion.102), channel_id=1, source_target_pairs={{0,16},{1,17},{2,18},{3,19},{4,20},{5,21},{6,22},{7,23},{8,24},{9,... | collective-permute-start | bytes 1572872 | tf_op jit(solution)/shard_map/ppermute | solution.py:74
  770.9 26.9 %collective-permute-start.36 = (bf16[512,512]{1,0:T(8,128)(2,1)S(1)}, bf16[512,512]{1,0:T(8,128)(2,1)S(1)}, u32[]{:S(2)}, u32[]{:S(2)}) collective-permute-start(bf16[512,512]{1,0:T(8,128)(2,1)S(1)} %fusion.101), channel_id=1, source_target_pairs={{0,16},{1,17},{2,18},{3,19},{4,20},{5,21},{6,22},{7,23},{8,24},{9,... | collective-permute-start | bytes 1572872 | tf_op jit(solution)/shard_map/ppermute | solution.py:74
  776.9 22.5 %collective-permute-start.48 = (bf16[256,1024]{1,0:T(8,128)(2,1)S(1)}, bf16[256,1024]{1,0:T(8,128)(2,1)S(1)}, u32[]{:S(2)}, u32[]{:S(2)}) collective-permute-start(bf16[256,1024]{1,0:T(8,128)(2,1)S(1)} %add_convert_fusion.5), channel_id=1, source_target_pairs={{0,8},{1,9},{2,10},{3,11},{4,12},{5,13},{6,14},{7,15},{8,0},{9,1},... | collective-permute-start | bytes 1572872 | tf_op jit(solution)/shard_map/ppermute | solution.py:74
  798.1 13.8 %collective-permute-start.37 = (bf16[512,512]{1,0:T(8,128)(2,1)S(1)}, bf16[512,512]{1,0:T(8,128)(2,1)S(1)}, u32[]{:S(2)}, u32[]{:S(2)}) collective-permute-start(bf16[512,512]{1,0:T(8,128)(2,1)S(1)} %add_convert_fusion.6), channel_id=1, source_target_pairs={{0,8},{1,9},{2,10},{3,11},{4,12},{5,13},{6,14},{7,15},{8,0},{9,1},... | collective-permute-start | bytes 1572872 | tf_op jit(solution)/shard_map/ppermute | solution.py:74
  (60 other events, 211.1 us)

commit v2 on v1

--- a/solution.py
+++ b/solution.py
@@ -614,6 +614,541 @@
     return (att, jnp.stack(halves))
 
 
+CHUNKS = 3
+PARTS = 4
+ORDER = (3, 1, 2, 0)
+
+
+def backward_kernel(
+    lengths,
+    x_ref,
+    gathered,
+    qkv_t,
+    qkv_s,
+    context_s,
+    slope_t,
+    slope_s,
+    hidden_s,
+    unit_t,
+    inverse_t,
+    unit_s,
+    inverse_s,
+    low_s,
+    grad_t,
+    grad_s,
+    vectors,
+    t_gain,
+    s_gain,
+    grad_in,
+    sums_out,
+    vec,
+    wide,
+    hidden_buf,
+    slope_buf,
+    qkv_s_buf,
+    qkv_t_buf,
+    context_buf,
+    extra_buf,
+    unit_buf,
+    inverse_buf,
+    grad_buf,
+    total,
+    low_y,
+    low_z,
+    low_a,
+    proj,
+    sums,
+    even,
+    odd,
+    from_core,
+    from_far,
+    from_x,
+    from_y,
+    from_z,
+    from_vec,
+    load,
+    state_sem,
+    odd_send,
+    odd_recv,
+    free,
+    far_send,
+    far_recv,
+    x_send,
+    x_recv,
+    y_send,
+    y_recv,
+    in_send,
+    in_recv,
+    mid_send,
+    mid_recv,
+    out_send,
+    out_recv,
+    vec_send,
+    vec_recv,
+    done,
+):
+    me = lax.axis_index("mp")
+    z = lax.axis_index("dp")
+    rows = x_ref.shape[0]
+    pairs = rows // LEN
+    core, along_x, along_y = ({"mp": flipped(me, bits)} for bits in (1, 2, 4))
+    z_outer, z_inner = {"dp": flipped(z, 1)}, {"dp": 3 - z}
+    z_two = {"dp": flipped(z, 2)}
+    inner = jnp.logical_or(z == 1, z == 2)
+    outer = jnp.logical_or(z == 0, z == 3)
+
+    barrier = pltpu.get_barrier_semaphore()
+    greeted = (core, along_x, along_y, z_outer, z_inner, z_two)
+    for peer in greeted:
+        pl.semaphore_signal(barrier, inc=1, device_id=peer, device_id_type=MESH)
+    pl.semaphore_wait(barrier, len(greeted))
+
+    def remote(src, dst, send, recv, peer):
+        return pltpu.make_async_remote_copy(
+            src_ref=src, dst_ref=dst, send_sem=send, recv_sem=recv, device_id=peer, device_id_type=MESH
+        )
+
+    steps = [("fs", 4 + half, pair) for half in range(2) for pair in ORDER]
+    steps += [("as", 1, pair) for pair in ORDER]
+    steps += [("ft", 2 + half, pair) for half in range(2) for pair in range(4)]
+    steps += [("at", 0, pair) for pair in range(4)]
+
+    def loads(number):
+        kind, pack, pair = steps[number]
+        place = number % 2
+        count = pack_rows(pack) if pack > 1 else FFN_ROWS
+        two = pl.ds(2 * pair, 2)
+        moves = [(gathered.at[pack, two, pl.ds(0, count)], wide.at[place, :, pl.ds(0, count)])]
+        if kind == "fs":
+            moves.append((hidden_s.at[pack - 4, pair], hidden_buf.at[place]))
+            moves.append((slope_s.at[pack - 4, pair], slope_buf.at[place]))
+        elif kind == "ft":
+            moves.append((slope_t.at[pack - 2, pair], slope_buf.at[place]))
+        else:
+            moves.append((qkv_t.at[two], qkv_t_buf.at[place]))
+            if kind == "as":
+                moves.append((qkv_s.at[two], qkv_s_buf.at[place]))
+                moves.append((context_s.at[pair], context_buf.at[place]))
+        return [
+            pltpu.make_async_copy(src, dst, load.at[place, index])
+            for index, (src, dst) in enumerate(moves)
+        ]
+
+    def state(layer):
+        unit, inverse, grad = ((unit_t, inverse_t, grad_t), (unit_s, inverse_s, grad_s))[layer]
+        moves = [(grad, grad_buf), (unit, unit_buf), (inverse, inverse_buf)]
+        return [
+            pltpu.make_async_copy(src, dst, state_sem.at[index])
+            for index, (src, dst) in enumerate(moves)
+        ]
+
+    def slot_row(slot):
+        row = me
+        for bits in (1, 2, 4):
+            if slot & bits:
+                row = flipped(row, bits)
+        return row
+
+    def odd_copy(number):
+        pair = steps[number][2]
+        return remote(
+            odd.at[number % 2], from_core.at[pair], odd_send.at[number % 2], odd_recv.at[pair], core
+        )
+
+    def keep(chunk, pair):
+        return sums.at[chunk] if pair == 0 else even.at[chunk, pair - 1]
+
+    def give(number, pieces):
+        pair = steps[number][2]
+        chunk = number // 4
+        if number >= 2:
+            odd_copy(number - 2).wait_send()
+        for start, values in pieces:
+            count = values.shape[0] // 2
+            keep(chunk, pair)[start : start + count] = to_low(values[:count])
+            odd[number % 2, start : start + count] = to_low(values[count:])
+        if chunk:
+            pl.semaphore_wait(free.at[pair], 1)
+        odd_copy(number).start()
+
+    def add_rows(target, others, start, count):
+        @pl.loop(0, count // 64)
+        def _(step):
+            here = pl.ds(start + step * 64, 64)
+            value = to_float(target[here])
+            for other in others:
+                value = value + to_float(other[here])
+            target[here] = to_low(value)
+
+    def combine(chunk, pair):
+        number = chunk * 4 + ORDER.index(pair)
+        odd_copy(number).wait_recv()
+        add_rows(keep(chunk, pair), [from_core.at[pair]], 0, FFN_ROWS)
+        if chunk < CHUNKS - 1:
+            pl.semaphore_signal(free.at[pair], inc=1, device_id=core, device_id_type=MESH)
+        if pair == 3:
+            far_copy(chunk, 0).start()
+            far_copy(chunk, 1).start()
+
+    def far_copy(chunk, way):
+        part = pl.ds(way * 256, 256)
+        return remote(
+            even.at[chunk, 2, part],
+            from_far.at[chunk, part],
+            far_send.at[chunk, way],
+            far_recv.at[chunk, way],
+            (along_x, along_y)[way],
+        )
+
+    part_rows = FFN_ROWS // PARTS
+
+    def plane_copies(chunk, part):
+        here = pl.ds(part * part_rows, part_rows)
+        return [
+            remote(even.at[chunk, 0, here], from_x.at[chunk, here], x_send.at[chunk, part], x_recv.at[chunk, part], along_x),
+            remote(even.at[chunk, 1, here], from_y.at[chunk, here], y_send.at[chunk, part], y_recv.at[chunk, part], along_y),
+        ]
+
+    def fold(chunk):
+        far_copy(chunk, 0).wait_recv()
+        add_rows(keep(chunk, 2), [from_far.at[chunk]], 0, 256)
+        far_copy(chunk, 1).wait_recv()
+        add_rows(keep(chunk, 1), [from_far.at[chunk]], 256, 256)
+        for part in range(PARTS):
+            for copy in plane_copies(chunk, part):
+                copy.start()
+
+    def z_copy(chunk, part, kind):
+        here = pl.ds(part * part_rows, part_rows)
+        own, first, second = sums.at[chunk, here], from_z.at[chunk, 0, here], from_z.at[chunk, 1, here]
+        if kind == 0:
+            return remote(own, first, in_send.at[chunk, part], in_recv.at[chunk, part], z_outer)
+        if kind == 1:
+            return remote(own, second, mid_send.at[chunk, part], mid_recv.at[chunk, part], z_inner)
+        return remote(first, first, out_send.at[chunk, part], out_recv.at[chunk, part], z_outer)
+
+    def own_part(chunk, part):
+        for copy in plane_copies(chunk, part):
+            copy.wait_recv()
+        add_rows(sums.at[chunk], [from_x.at[chunk], from_y.at[chunk]], part * part_rows, part_rows)
+
+        @pl.when(outer)
+        def _():
+            z_copy(chunk, part, 0).start()
+
+    def mid_part(chunk, part):
+        @pl.when(inner)
+        def _():
+            z_copy(chunk, part, 0).wait_recv()
+            add_rows(sums.at[chunk], [from_z.at[chunk, 0]], part * part_rows, part_rows)
+            z_copy(chunk, part, 1).start()
+
+    def end_part(chunk, part):
+        @pl.when(inner)
+        def _():
+            z_copy(chunk, part, 1).wait_recv()
+
+            @pl.loop(0, part_rows // 64)
+            def _(step):
+                here = pl.ds(part * part_rows + step * 64, 64)
+                value = to_float(sums[chunk, here]) + to_float(from_z[chunk, 1, here])
+                from_z[chunk, 0, here] = to_low(value)
+
+            z_copy(chunk, part, 2).start()
+
+    def store_copy(chunk):
+        return pltpu.make_async_copy(from_z.at[chunk, 0], sums_out.at[chunk], done.at[chunk])
+
+    def finish(chunk):
+        @pl.when(outer)
+        def _():
+            for part in range(PARTS):
+                z_copy(chunk, part, 2).wait_recv()
+
+        store_copy(chunk).start()
+
+    ways = (core, along_x, along_y, z_outer, z_two)
+
+    def vec_copy(way):
+        return remote(vec, from_vec.at[way], vec_send.at[way], vec_recv.at[way], ways[way])
+
+    def vec_add(way):
+        vec_copy(way).wait_send()
+        vec_copy(way).wait_recv()
+        vec[...] += from_vec[way]
+        if way + 1 < len(ways):
+            vec_copy(way + 1).start()
+
+    def put_bias(pair, start, values):
+        count = values.shape[1] // 2
+        for side in range(2):
+            line = lax.broadcasted_iota(jnp.int32, (SLOTS, count), 0)
+            part = jnp.broadcast_to(values[:, side * count : (side + 1) * count], (SLOTS, count))
+            part = jnp.where(line == slot_row(2 * pair + side), part, 0.0)
+            vec[0:SLOTS, start : start + count] += part
+
+    def ffn_step(number):
+        kind, pack, pair = steps[number]
+        place = number % 2
+        up = wide[place, :, 0:HALF_UNITS].reshape(2 * HALF_UNITS, -1)
+        down = wide[place, :, HALF_UNITS : 2 * HALF_UNITS].reshape(2 * HALF_UNITS, -1)
+        back = dot_nt(low_z[...], down) * to_float(slope_buf[place])
+        back_low = to_low(back)
+        total[...] += dot(back_low, up)
+        if kind == "fs":
+            put_bias(pair, 2 * COLS + (pack - 4) * HALF_UNITS, jnp.sum(back, axis=0, keepdims=True))
+            up_grad = dot_tn(back_low, low_y[...])
+            down_grad = dot_tn(hidden_buf[place], low_z[...])
+            give(number, [(0, up_grad), (HALF_UNITS, down_grad)])
+
+    def pick(both):
+        first = lax.broadcasted_iota(jnp.int32, (LEN, COLS), 1) < DH
+        return jnp.where(first, both[:LEN], both[LEN:])
+
+    def attention_step(number):
+        kind, pack, pair = steps[number]
+        place = number % 2
+        student = kind == "as"
+        factor = 1.0 / math.sqrt(DH)
+        qkv = qkv_s_buf if student else qkv_t_buf
+        out = wide[place, :, 384:512].reshape(2 * COLS, -1)
+        context_back = to_low(dot_nt(low_a[...], out))
+        query_sums, value_sums = [], []
+        for side in range(2):
+            query_sum = jnp.zeros((1, COLS), jnp.float32)
+            value_sum = jnp.zeros((1, COLS), jnp.float32)
+            for number_b in range(pairs):
+                here = slice(number_b * LEN, (number_b + 1) * LEN)
+                length = lengths[me * pairs + number_b]
+                query, key, value = [
+                    qkv[place, side, here, i * COLS : (i + 1) * COLS] for i in range(3)
+                ]
+                keys, values = two_heads(key), two_heads(value)
+                scores = dot_nt(query, keys) * factor
+                probs = masked_probs(scores, length)
+                if student:
+                    other = dot_nt(
+                        qkv_t_buf[place, side, here, 0:COLS],
+                        two_heads(qkv_t_buf[place, side, here, COLS : 2 * COLS]),
+                    )
+                    spot = lax.broadcasted_iota(jnp.int32, scores.shape, 1)
+                    spot = jnp.where(spot < LEN, spot, spot - LEN)
+                    line = lax.broadcasted_iota(jnp.int32, scores.shape, 0)
+                    gap = score_weight * (scores - other * factor)
+                    extra = jnp.where(jnp.maximum(spot, line) < length, gap, 0.0)
+                    extra_buf[pair, side, number_b] = to_low(extra)
+                else:
+                    extra = -to_float(extra_buf[pair, side, number_b])
+                part = context_back[here, side * COLS : (side + 1) * COLS]
+                probs_back = dot_nt(part, values)
+                value_back = pick(dot_tn(to_low(probs), part))
+                product = probs * probs_back
+                inner_sum = jnp.concatenate(
+                    [
+                        jnp.broadcast_to(
+                            jnp.sum(product[:, i * LEN : (i + 1) * LEN], axis=1, keepdims=True), (LEN, LEN)
+                        )
+                        for i in range(2)
+                    ],
+                    axis=1,
+                )
+                score_back = to_low(product - probs * inner_sum + extra)
+                query_back = dot(score_back, keys) * factor
+                key_back = pick(dot_tn(score_back, query)) * factor
+                start = side * 3 * COLS
+                proj[here, start : start + COLS] = to_low(query_back)
+                proj[here, start + COLS : start + 2 * COLS] = to_low(key_back)
+                proj[here, start + 2 * COLS : start + 3 * COLS] = to_low(value_back)
+                if student:
+                    query_sum += jnp.sum(query_back, axis=0, keepdims=True)
+                    value_sum += jnp.sum(value_back, axis=0, keepdims=True)
+            query_sums.append(query_sum)
+            value_sums.append(value_sum)
+        grad_in[...] += dot(proj[...], wide[place, :, 0:384].reshape(768, -1))
+        if student:
+            put_bias(pair, 0, jnp.concatenate(query_sums, axis=1))
+            put_bias(pair, COLS, jnp.concatenate(value_sums, axis=1))
+            qkv_grad = dot_tn(proj[...], x_ref[...])
+            out_grad = dot_tn(context_buf[place], low_a[...])
+            give(number, [(0, qkv_grad), (3 * COLS, out_grad)])
+
+    def lower_grad():
+        @pl.loop(0, rows // 64)
+        def _(step):
+            here = pl.ds(step * 64, 64)
+            low_z[here] = to_low(grad_buf[here])
+
+        total[...] = jnp.zeros_like(total)
+
+    def norm_step(student):
+        gain_ref = s_gain if student else t_gain
+
+        @pl.loop(0, rows // 64)
+        def _(step):
+            here = pl.ds(step * 64, 64)
+            grad = grad_buf[here] + total[here]
+            unit = unit_buf[here]
+            back = norm_back(grad, unit, inverse_buf[here], to_float(gain_ref[0:1]))
+            low_a[here] = to_low(back)
+            if student:
+                grad_in[here] = back
+                vec[8:9] += jnp.sum(back, axis=0, keepdims=True)
+                vec[9:10] += jnp.sum(grad * unit, axis=0, keepdims=True)
+                vec[10:11] += jnp.sum(grad, axis=0, keepdims=True)
+            else:
+                grad_in[here] += back
+
+    hooks = {
+        1: [(combine, 0, 3)],
+        2: [(combine, 0, 1)],
+        3: [(combine, 0, 2)],
+        4: [(combine, 0, 0)],
+        5: [(combine, 1, 3)],
+        6: [(combine, 1, 1)],
+        7: [(combine, 1, 2), (fold, 0)],
+        8: [(combine, 1, 0)],
+        9: [(combine, 2, 3), (fold, 1)],
+        10: [(combine, 2, 1)],
+        11: [(combine, 2, 2)],
+        12: [(combine, 2, 0)],
+        13: [(own_part, 0, 0), (own_part, 0, 1)],
+        14: [(own_part, 0, 2), (own_part, 0, 3), (vec_add, 0)],
+        16: [(vec_add, 1)],
+        18: [(mid_part, 0, 0), (vec_add, 2)],
+        19: [(mid_part, 0, 1)],
+        20: [(mid_part, 0, 2), (mid_part, 0, 3), (vec_add, 3)],
+        21: [(end_part, 0, 0), (end_part, 0, 1), (vec_add, 4)],
+        22: [(end_part, 0, 2), (end_part, 0, 3), (own_part, 1, 0), (own_part, 1, 1)],
+        23: [(own_part, 1, 2), (own_part, 1, 3), (fold, 2), (mid_part, 1, 0), (mid_part, 1, 1)],
+    }
+
+    for copy in state(1):
+        copy.start()
+    low_copy = pltpu.make_async_copy(low_s, low_y, state_sem.at[3])
+    low_copy.start()
+    for copy in loads(0):
+        copy.start()
+    vec[...] = jnp.zeros_like(vec)
+    vec[11:14] = vectors[0:3]
+    for copy in state(1):
+        copy.wait()
+    low_copy.wait()
+    lower_grad()
+    for number, (kind, pack, pair) in enumerate(steps):
+        for copy in loads(number):
+            copy.wait()
+        if number + 1 < len(steps):
+            for copy in loads(number + 1):
+                copy.start()
+        if kind in ("fs", "ft"):
+            ffn_step(number)
+        else:
+            attention_step(number)
+        for action, *which in hooks.get(number, ()):
+            action(*which)
+        if number == 7:
+            norm_step(True)
+            for copy in state(0):
+                copy.start()
+        elif number == 11:
+            for copy in state(0):
+                copy.wait()
+            lower_grad()
+            vec_copy(0).start()
+        elif number == 19:
+            norm_step(False)
+    mid_part(1, 2)
+    mid_part(1, 3)
+    for part in range(PARTS):
+        end_part(1, part)
+    finish(0)
+    for part in range(PARTS):
+        own_part(2, part)
+        mid_part(2, part)
+    finish(1)
+    for part in range(PARTS):
+        end_part(2, part)
+    finish(2)
+
+    odd_copy(10).wait_send()
+    odd_copy(11).wait_send()
+    for chunk in range(CHUNKS):
+        far_copy(chunk, 0).wait_send()
+        far_copy(chunk, 1).wait_send()
+        for part in range(PARTS):
+            for copy in plane_copies(chunk, part):
+                copy.wait_send()
+
+            @pl.when(outer)
+            def _():
+                z_copy(chunk, part, 0).wait_send()
+
+            @pl.when(inner)
+            def _():
+                z_copy(chunk, part, 1).wait_send()
+                z_copy(chunk, part, 2).wait_send()
+
+        store_copy(chunk).wait()
+
+
+def backward_both(lengths, tokens, kept, vectors, t_gain, s_gain):
+    rows, features = tokens.shape
+    low, full = jnp.bfloat16, jnp.float32
+    vmem = pl.BlockSpec(memory_space=pltpu.VMEM)
+    hbm = pl.BlockSpec(memory_space=pl.ANY)
+    dma = pltpu.SemaphoreType.DMA
+    block = (FFN_ROWS, features)
+    return pl.pallas_call(
+        backward_kernel,
+        out_shape=[
+            jax.ShapeDtypeStruct((rows, features), full),
+            jax.ShapeDtypeStruct((CHUNKS,) + block, low),
+            jax.ShapeDtypeStruct((16, features), full),
+        ],
+        in_specs=[pl.BlockSpec(memory_space=pltpu.SMEM), vmem] + [hbm] * len(kept) + [vmem] * 3,
+        out_specs=[vmem, hbm, vmem],
+        scratch_shapes=[
+            pltpu.VMEM((2, 2) + block, low),
+            pltpu.VMEM((2, rows, 2 * HALF_UNITS), low),
+            pltpu.VMEM((2, rows, 2 * HALF_UNITS), low),
+            pltpu.VMEM((2, 2, rows, 3 * COLS), low),
+            pltpu.VMEM((2, 2, rows, 3 * COLS), low),
+            pltpu.VMEM((2, rows, 2 * COLS), low),
+            pltpu.VMEM((4, 2, rows // LEN, LEN, 2 * LEN), low),
+            pltpu.VMEM((rows, features), full),
+            pltpu.VMEM((rows, 1), full),
+            pltpu.VMEM((rows, features), full),
+            pltpu.VMEM((rows, features), full),
+            pltpu.VMEM((rows, features), low),
+            pltpu.VMEM((rows, features), low),
+            pltpu.VMEM((rows, features), low),
+            pltpu.VMEM((rows, 6 * COLS), low),
+            pltpu.VMEM((CHUNKS,) + block, low),
+            pltpu.VMEM((CHUNKS, 3) + block, low),
+            pltpu.VMEM((2,) + block, low),
+            pltpu.VMEM((4,) + block, low),
+            pltpu.VMEM((CHUNKS,) + block, low),
+            pltpu.VMEM((CHUNKS,) + block, low),
+            pltpu.VMEM((CHUNKS,) + block, low),
+            pltpu.VMEM((CHUNKS, 2) + block, low),
+            pltpu.VMEM((5, 16, features), full),
+            dma((2, 4)),
+            dma((4,)),
+            dma((2,)),
+            dma((4,)),
+            pltpu.SemaphoreType.REGULAR((4,)),
+            dma((CHUNKS, 2)),
+            dma((CHUNKS, 2)),
+        ]
+        + [dma((CHUNKS, PARTS))] * 10
+        + [dma((5,)), dma((5,)), dma((CHUNKS,))],
+        compiler_params=pltpu.CompilerParams(
+            collective_id=1, has_side_effects=True, vmem_limit_bytes=63 * 1024 * 1024
+        ),
+        name="backward_both",
+    )(lengths, tokens, *kept, vectors, t_gain, s_gain)
+
+
 def cut(values, count, axis):
     return jnp.split(values, count, axis=axis)
 
@@ -673,27 +1208,28 @@
             (teacher_out_bias, teacher_gain, teacher_shift),
             (student_out_bias, student_gain, student_shift),
         )
-        def unpack(layer):
-            att = gathered[layer]
-            qkvt = att[:, :384].reshape(8, 3, 128, -1)
-            qkv = [qkvt[:, i].reshape(1024, -1).T for i in range(3)]
-            out = att[:, 384:512].reshape(1024, -1)
-            f = gathered[2 + 2 * layer : 4 + 2 * layer]
-            up = f[:, :, 0:256].transpose(1, 0, 2, 3).reshape(4096, -1).T
-            down = f[:, :, 256:512].transpose(1, 0, 2, 3).reshape(4096, -1)
-            return (qkv, None, None, out, up, None, down)
-        def spread(v):
-            return v.reshape(2, 4, rows, 2, 256).transpose(2, 1, 3, 0, 4).reshape(rows, 4096)
-        def keep(qkv, slope, hidden, unit, inverse, low, context):
-            q, k, v = [qkv[:, :, i * 128:(i + 1) * 128].transpose(1, 0, 2).reshape(pairs, LEN, 16, 64) for i in range(3)]
-            scores = jnp.einsum("bqhe,bkhe->bhqk", q, k, preferred_element_type=jnp.float32) * (1.0 / math.sqrt(DH))
-            masked = jnp.where(valid[:, None, None, :], scores, masked_fill)
-            attention = jax.nn.softmax(masked, axis=-1)
-            return [q, k, v, scores, attention, context, unit, inverse, low, hidden, spread(slope), None, None]
-        teach, stud = unpack(0), unpack(1)
-        ctx = context_s.transpose(1, 0, 2).reshape(rows, -1)
-        teach_kept = keep(qkv_t, slope_t, None, unit_t, inverse_t, None, None)
-        kept = keep(qkv_s, slope_s, spread(hidden_s), unit_s, inverse_s, low_s, ctx)
+        input_grad, sums, vec = backward_both(
+            lengths, tokens,
+            (gathered, qkv_t, qkv_s, context_s, slope_t, slope_s, hidden_s, unit_t, inverse_t, unit_s,
+             inverse_s, low_s, grad_t, grad_s),
+            vecs, teacher_gain, student_gain,
+        )
+        sums = to_float(sums)
+        row = lax.dynamic_slice_in_dim(vec, me, 1)[0]
+        features = tokens.shape[1]
+        return (
+            student_output,
+            input_grad,
+            sums[2, : 3 * COLS].reshape(3, COLS, features).transpose(2, 0, 1),
+            row[: 2 * COLS].reshape(2, COLS),
+            sums[2, 3 * COLS :],
+            sums[:2, :HALF_UNITS].reshape(2 * HALF_UNITS, features).T,
+            row[2 * COLS : 2 * COLS + 2 * HALF_UNITS],
+            sums[:2, HALF_UNITS:].reshape(2 * HALF_UNITS, features),
+            jnp.stack([vec[8], vec[11]]),
+            jnp.stack([vec[9], vec[12]]),
+            jnp.stack([vec[10], vec[13]]),
+        )
     else:
         teach = gather_layer(
             net, teacher_qkv, teacher_qv_bias, teacher_out, teacher_up, teacher_up_bias, teacher_down

time: 822 us -> 475 us (0.58)
  Pallas kernels: 230 us -> 430 us
  local copies, waits for them, and re-layouts: 223 us -> 27.4 us
  waiting for transfers between devices: 154 us -> 0 us
  matrix products: 121 us -> 0 us
  other arithmetic: 53.9 us -> 12.1 us
  starting transfers between devices: 30.9 us -> 0 us
    pallas_call x0 -> x1, Pallas kernels: none -> 201 us  [backward_both(): pl.pallas_call(backward_kernel, out_shape=[jax.ShapeDtypeStruct((rows, fe...]
    ppermute x49 -> x0, waiting for transfers between devices: 154 us -> none  [the longest x14 79 us: flip_dp(): return lax.ppermute(values, self.axes, pairs)]
    dot_general x28 -> x0, matrix products: 121 us -> none  [the longest x12 47.7 us: dot_nt(): lax.dot_general(left, right, (((1,), (1,)), ((), ())), preferred_element_...]
    transpose x14 -> x0, local copies, waits for them, and re-layouts: 70.5 us -> none  [the longest x3 39.1 us: unpack(): down = f[:, :, 256:512].transpose(1, 0, 2, 3).reshape(4096, -1)]
    convert_element_type x15 -> x0, local copies, waits for them, and re-layouts: 50.3 us -> none  [the longest x5 43.5 us: backward_ffn(): pre_grad = dot_nt(second_low, down) * slope]
    reshape x12 -> x1, local copies, waits for them, and re-layouts: 38.8 us -> 2.88 us  [per_device(): sums[:2, :HALF_UNITS].reshape(2 * HALF_UNITS, features)]
    ppermute x49 -> x0, starting transfers between devices: 30.9 us -> none  [the longest x35 20.3 us: flip(): return lax.ppermute(values, self.axes, pairs)]
    add x13 -> x0, other arithmetic: 14.3 us -> none  [the longest x4 8.8 us: scatter(): to_float(blocks[k]) + to_float(self.flip(blocks[k + 1], 1))]
  transfers between devices with their start and end apart: 49 -> 0, of which waited for: 19 -> 0; matrix products, arithmetic and copies ran while one was open for 43% -> 0% of each run, Pallas kernels for 0% -> 0%
where the time goes in v2:
time: 475 us; the launch traced here: 471 us
  Pallas kernels  430 us (91%)
  local copies, waits for them, and re-layouts  27.4 us (6%)
  other arithmetic  12.1 us (3%)
    pallas_call x1, Pallas kernels, forward_both(): pl.pallas_call(forward_kernel, out_shape=[jax.ShapeDtypeStruct(shape, kin...  230 us
    pallas_call x1, Pallas kernels, backward_both(): pl.pallas_call(backward_kernel, out_shape=[jax.ShapeDtypeStruct((rows, fe...  201 us
    unnamed x39, local copies, waits for them, and re-layouts  10.9 us

profile of v2, /device:TPU:0, one launch (start us, length us, event | category | flops | bytes accessed | tf_op | source)
XLA Modules:
  0.0 471.1 jit_solution(3689095714270560479)
XLA Ops:
  0.6 0.0 copy-start.1
  0.7 3.0 copy.35
  3.7 0.0 copy-done.1
  3.7 0.3 abs_reduce_fusion.1
  4.0 1.3 copy-done.3
  5.3 0.6 multiply_convert_fusion.1
  5.9 0.1 slice_bitcast_fusion.2
  5.9 0.9 copy-done.2
  6.9 0.2 abs_reduce_fusion
  7.1 0.6 multiply_convert_fusion
  7.7 0.1 fusion.10
  7.8 0.0 copy-start.9
  7.8 0.2 maximum_bitcast_fusion.2
  8.0 1.0 copy-done.9
  9.0 0.1 fusion.8
  9.1 1.0 copy.39
  10.1 1.0 copy.38
  11.1 1.3 fusion.9
  12.4 0.0 copy-done.6
  12.4 0.0 copy-done.7
  12.5 0.2 maximum_bitcast_fusion
  12.6 0.0 copy-start.4
  12.6 2.7 pad_maximum_fusion.packs_ffn
  15.4 0.0 copy-done.4
  15.4 0.2 abs_reduce_fusion.2
  15.6 0.0 copy-start.10
  15.6 0.5 fusion.6
  16.0 0.0 copy-start.5
  16.1 0.0 copy-start.13
  16.1 0.0 copy-start.15
  16.1 0.0 copy-start.14
  16.1 0.0 copy-start.16
  16.1 0.0 copy-start.12
  16.1 0.3 copy.32
  16.4 0.3 copy-done.10
  16.7 0.3 copy.31
  17.0 0.2 copy-done.5
  17.2 0.1 abs_reduce_fusion.3
  17.3 0.2 multiply_convert_fusion.3
  17.4 0.0 copy-done.13
  17.4 0.0 copy-done.15
  17.5 0.0 copy-done.14
  17.5 0.0 copy-done.16
  17.5 0.0 copy-done.12
  17.5 0.2 fusion.3
  17.8 1.6 pad_maximum_fusion.1.packs_att
  19.4 229.6 %forward_both.1 = (bf16[6,8,528,1024]{3,2,1,0:T(8,128)(2,1)}, bf16[8,384,384]{2,1,0:T(8,128)(2,1)}, bf16[8,384,384]{2,1,0:T(8,128)(2,1)}, bf16[4,384,256]{2,1,0:...) custom-call(s32[24]{0:T(128)} %lengths.3, ...), custom_call_target="tpu_custom_call" | custom-call | tf_op jit(solution)/shard_map/forward_both/pallas_call | solution.py:572
  249.0 200.8 %backward_both.1 = (f32[384,1024]{1,0:T(8,128)}, bf16[3,512,1024]{2,1,0:T(8,128)(2,1)}, f32[16,1024]{1,0:T(8,128)}) custom-call(s32[24]{0:T(128)} %lengths.3, bf16[384,1024]{1,0:T(8,128)(2,1)} %x_ref.3, bf16[6,8,528,1024]{3,2,1,0:T(8,128)(2,1)} %get-tuple-element.31.gathered, bf16[8,384,384]{2,1,0:T(8,128)(2,1)} %get-tuple-element.32.qkv_t, ...), custom_call_target="tpu_custom_call" | custom-call | tf_op jit(solution)/shard_map/backward_both/pallas_call | solution.py:1101
  449.8 1.1 fusion.11
  450.9 0.6 pad_maximum_fusion.4
  451.5 0.6 pad_maximum_fusion.3
  452.1 0.6 pad_maximum_fusion.2
  452.8 2.8 convert_element_type.22
  455.5 0.8 slice_bitcast_fusion
  456.4 0.0 copy-done
  456.4 2.5 fusion.7
  458.9 2.9 copy.37
  461.8 1.3 slice.89
  463.1 3.2 copy.36
  466.2 1.4 dynamic-slice.1
  467.6 1.3 constant_dynamic-slice_fusion
  468.9 0.9 copy.42
  469.8 0.0 copy-done.8
  469.8 1.1 copy.43
  (16 shorter events, 0.1 us)
Async XLA Ops:
  0.6 3.0 copy-start.1
  3.7 1.6 copy-start.3
  5.3 1.6 copy-start.2
  7.8 1.2 copy-start.9
  10.1 2.3 copy-start.6
  11.1 1.4 copy-start.7
  12.6 2.8 copy-start.4
  15.6 1.1 copy-start.10
  16.0 1.1 copy-start.5
  16.1 1.4 copy-start.13
  16.1 1.4 copy-start.15
  16.1 1.4 copy-start.14
  16.1 1.4 copy-start.16
  16.1 1.4 copy-start.12
  452.8 3.6 copy-start
  463.1 5.8 %copy-start.11 = (bf16[384,1024]{1,0:T(8,128)(2,1)S(1)}, bf16[384,1024]{1,0:T(8,128)(2,1)}, u32[]{:S(2)}) copy-start(bf16[384,1024]{1,0:T(8,128)(2,1)} %get-tuple-element.82) | copy-start | bytes 2359300
  463.1 6.7 %copy-start.8 = (f32[384,1024]{1,0:T(8,128)S(1)}, f32[384,1024]{1,0:T(8,128)}, u32[]{:S(2)}) copy-start(f32[384,1024]{1,0:T(8,128)} %get-tuple-element.83) | copy-start | bytes 4718596
